TPU v7x, 128 devices: a whole 4x4x4 slice. The times are simulated.
128 devices in a mesh: lat: 4 (over z_hi, core), lon: 32 (over x, y, z_lo).
Axes of the slice: x: 4, y: 4, z: 4 (z_hi: 2, z_lo: 2; z = z_hi * 2 + z_lo), core: 2. Of those that a mesh axis runs over, the one named last changes fastest.
Arguments:
- coarse: bfloat16 [384, 1024, 384], P('lat', 'lon'), may hold values from -6 to 6
- ocean_tiles: int32 [12, 32], P('lat', 'lon'), may hold values from 0 to 1, as said below
- dw_weight: float32 [2, 7, 7, 384], replicated, may hold values from -0.875 to 0.875
- dw_bias: float32 [2, 384], replicated, may hold values from -3 to 3
- norm_gain: float32 [2, 384], replicated, may hold values from 0.5 to 1.5
- norm_shift: float32 [2, 384], replicated, may hold values from -3 to 3
- in_weight: bfloat16 [2, 384, 768], replicated, may hold values from -0.3125 to 0.3125
- in_bias: float32 [2, 768], replicated, may hold values from -3 to 3
- out_weight: bfloat16 [2, 768, 384], replicated, may hold values from -0.21875 to 0.21875
- out_bias: float32 [2, 384], replicated, may hold values from -3 to 3
- layer_scale: float32 [2, 384], replicated, may hold values from 0.3 to 1
- up_weight: bfloat16 [3, 3, 384, 192], replicated, may hold values from -0.15625 to 0.15625
- up_bias: float32 [192], replicated, may hold values from -3 to 3
Outputs:
- fine: bfloat16 [768, 2048, 192], P(('lat', 'lon'))
Inputs may be any that keep to these rules, and one draw needn't show every extreme that they name: `ocean_tiles`: 1 marks a tile with ocean, 0 an all-land tile. The tiles are partitioned evenly: each aligned block of 3 by 1 tiles (those of one device) holds exactly max(1, K // 3) land tiles, with K the tiles of the block.
All inputs are finite; a program needn't handle non-finite values.
Results may differ from a plain program's by a relative error of at most 0.0075.
Values may be sent and summed in bfloat16 or wider, within the bound.
A program may use at most 128 MiB of HBM per device.

v0:
```python
import jax
import jax.numpy as jnp
from jax import lax
from jax.sharding import PartitionSpec as P

LAYERS = 2
TS = 32


def padded_2(x, sides, width, wrap):
    for axis, dim in sides:
        size, length = (lax.axis_size(axis), x.shape[dim])
        up = [(i, (i + 1) % size) for i in range(size if wrap else size - 1)]
        down = [(j, i) for i, j in up]
        last = lax.slice_in_dim(x, length - width, length, axis=dim)
        initial = lax.slice_in_dim(x, 0, width, axis=dim)
        before = lax.ppermute(last, axis, up)
        after = lax.ppermute(initial, axis, down)
        x = jnp.concatenate([before, x, after], axis=dim)
    return x


def shifted(value, axis, steps):
    count = lax.axis_size(axis)
    pairs = [(source, (source + steps) % count) for source in range(count)]
    return lax.ppermute(value, axis, pairs)


def passed_along(block, axis, distance):
    devices = range(lax.axis_size(axis))
    route = [(i - distance, i) for i in devices if i - distance in devices]
    return lax.ppermute(block, axis, route)


def depthwise(padded, weights, bias, row_count, column_count):
    total = jnp.zeros((row_count, column_count, padded.shape[2]), jnp.float32)
    for row_tap in range(7):
        for column_tap in range(7):
            window = padded[row_tap : row_tap + row_count, column_tap : column_tap + column_count]
            total = total + window.astype(jnp.float32) * weights[row_tap, column_tap]
    return total + bias


def mixer(depth, gain, shift, in_weight, in_bias, out_weight, out_bias):
    channels = depth.shape[-1]
    center = jnp.mean(depth, -1, keepdims=True)
    offset = depth - center
    spread = jnp.mean(offset * offset, -1, keepdims=True)
    normed = (offset * lax.rsqrt(spread + 1e-06) * gain + shift).astype(jnp.bfloat16)
    flat = normed.reshape(-1, channels)
    hidden = jax.nn.gelu(
        jnp.dot(flat, in_weight, preferred_element_type=jnp.float32) + in_bias, approximate=True
    ).astype(jnp.bfloat16)
    result = jnp.dot(hidden, out_weight, preferred_element_type=jnp.float32) + out_bias
    return result.reshape(depth.shape)


def upsample(extended, weight, bias):
    row_count = extended.shape[0] - 1
    column_count = extended.shape[1] - 1
    channels = extended.shape[2]
    width_out = weight.shape[3]
    current_cell = extended[:-1, :-1].reshape(-1, channels)
    right_cell = extended[:-1, 1:].reshape(-1, channels)
    lower_cell = extended[1:, :-1].reshape(-1, channels)
    corner_cell = extended[1:, 1:].reshape(-1, channels)
    direct = jnp.dot(
        current_cell,
        jnp.concatenate([weight[1, 1], weight[1, 2], weight[2, 1], weight[2, 2]], 1),
        preferred_element_type=jnp.float32,
    )
    beside = jnp.dot(
        right_cell,
        jnp.concatenate([weight[1, 0], weight[2, 0]], 1),
        preferred_element_type=jnp.float32,
    )
    beneath = jnp.dot(
        lower_cell,
        jnp.concatenate([weight[0, 1], weight[0, 2]], 1),
        preferred_element_type=jnp.float32,
    )
    diagonal_term = jnp.dot(corner_cell, weight[0, 0], preferred_element_type=jnp.float32)
    phase_even_even = direct[:, :width_out]
    phase_even_odd = direct[:, width_out : 2 * width_out] + beside[:, :width_out]
    phase_odd_even = direct[:, 2 * width_out : 3 * width_out] + beneath[:, :width_out]
    phase_odd_odd = (
        direct[:, 3 * width_out :] + beside[:, width_out:] + beneath[:, width_out:] + diagonal_term
    )
    upper_rows = jnp.stack([phase_even_even, phase_even_odd], 1).reshape(
        row_count, 2 * column_count, width_out
    )
    bottom_rows = jnp.stack([phase_odd_even, phase_odd_odd], 1).reshape(
        row_count, 2 * column_count, width_out
    )
    whole = jnp.stack([upper_rows, bottom_rows], 1).reshape(
        2 * row_count, 2 * column_count, width_out
    )
    return (whole + bias).astype(jnp.bfloat16)


def local(
    coarse,
    ocean_tiles,
    dw_weight,
    dw_bias,
    norm_gain,
    norm_shift,
    in_weight,
    in_bias,
    out_weight,
    out_bias,
    layer_scale,
    up_weight,
    up_bias,
):
    height = coarse.shape[0]
    width = coarse.shape[1]
    tile_rows = ocean_tiles.shape[0]
    tile_cols = ocean_tiles.shape[1]
    ocean_float = ocean_tiles.astype(jnp.float32)
    cell_mask = jnp.broadcast_to(
        ocean_float[:, None, :, None], (tile_rows, TS, tile_cols, TS)
    ).reshape(height, width)
    field = coarse
    for layer_index in range(LAYERS):
        widened = padded_2(field, (("lon", 1),), 3, True)
        padded = padded_2(widened, (("lat", 0),), 3, False)
        params = (
            norm_gain[layer_index],
            norm_shift[layer_index],
            in_weight[layer_index],
            in_bias[layer_index],
            out_weight[layer_index],
            out_bias[layer_index],
        )
        depth = depthwise(padded, dw_weight[layer_index], dw_bias[layer_index], height, width)
        update = mixer(depth, *params)
        field = (
            field.astype(jnp.float32) + cell_mask[..., None] * layer_scale[layer_index] * update
        ).astype(jnp.bfloat16)
    column_next = shifted(field[:, :1], "lon", -1)
    widened_field = jnp.concatenate([field, column_next], 1)
    row_next = passed_along(widened_field[:1], "lat", -1)
    extended = jnp.concatenate([widened_field, row_next], 0)
    local_fine = upsample(extended, up_weight, up_bias)
    return lax.all_to_all(local_fine, "lon", split_axis=0, concat_axis=1, tiled=True)


def solution(mesh):
    placed = (
        P("lat", "lon", None),
        P("lat", "lon"),
        P(),
        P(),
        P(),
        P(),
        P(),
        P(),
        P(),
        P(),
        P(),
        P(),
        P(),
    )
    return jax.shard_map(
        local, mesh=mesh, in_specs=placed, out_specs=P(("lat", "lon"), None, None), check_vma=False
    )
```

profile of v0, /device:TPU:1, one launch (start us, length us, event | category | flops | bytes accessed | tf_op | source)
XLA Modules:
  0.0 357.1 jit_solution(17865329261946061753)
XLA Ops:
  1.7 7.2 %collective-permute-start.1 = (bf16[96,3,384]{2,0,1:T(8,128)(2,1)S(1)}, bf16[96,3,384]{2,0,1:T(8,128)(2,1)S(1)}, u32[]{:S(2)}, u32[]{:S(2)}) collective-permute-start(bf16[96,3,384]{2,0,1:T(8,128)(2,1)S(1)} %copy.64), channel_id=1, source_target_pairs={{1,0},{2,1},{3,2},{4,3},{5,4},{6,5},{7,6},{8,7},{9,8},{10,9},{11,1... | collective-permute-start | bytes 663560 | tf_op jit(solution)/shard_map/ppermute | solution.py:18
  21.0 6.8 %collective-permute-start.2 = (bf16[3,38,384]{2,1,0:T(8,128)(2,1)S(1)}, bf16[3,38,384]{2,1,0:T(8,128)(2,1)S(1)}, u32[]{:S(2)}, u32[]{:S(2)}) collective-permute-start(bf16[3,38,384]{2,1,0:T(8,128)(2,1)S(1)} %get-tuple-element.130), channel_id=1, source_target_pairs={{0,32},{32,64},{64,96},{1,33},{33,65},{65,97},{2,34},{34,66},{66,9... | collective-permute-start | bytes 262664 | tf_op jit(solution)/shard_map/ppermute | solution.py:17
  31.6 3.6 collective-permute-done.3
  35.2 3.4 maximum_maximum_fusion
  38.7 36.5 %fusion.124 = (f32[96,32]{1,0:T(8,128)S(1)}, f32[96,32,384]{2,1,0:T(8,128)S(1)}) fusion(f32[384]{0:T(512)S(1)} %copy-done.50, f32[384]{0:T(512)S(1)} %get-tuple-element.55, bf16[99,38,384]{2,1,0:T(8,128)(2,1)S(1)} %get-tuple-element.129, f32[384]{0:T(512)S(1)} %get-tuple-element.56, f32[384]{0:T(512)S(1)} %get-tuple-element.57, ...), kind=kLoop, calls=%fused_computation.297 | loop fusion | flops 185201664 | bytes 113556480 | tf_op jit(solution)/shard_map/reduce_sum | solution.py:46
  78.3 9.1 %convolution_add_fusion.1 = f32[3072,384]{1,0:T(8,128)} fusion(f32[384]{0:T(512)S(1)} %copy-done.57, bf16[3072,384]{1,0:T(8,128)(2,1)} %bitcast.78, f32[768]{0:T(1024)S(1)} %copy-done.55, bf16[2,768,384]{2,1,0:T(8,128)(2,1)} %param.21, bf16[2,384,768]{2,1,0:T(8,128)(2,1)} %param.19), kind=kOutput, calls=%fused_computation.86 | convolution fusion | flops 3648651264 | bytes 8262144 | tf_op jit(solution)/shard_map/dot_general | solution.py:54
  87.4 3.1 fusion.42
  90.8 4.6 %collective-permute-start.5 = (bf16[96,3,384]{2,0,1:T(8,128)(2,1)S(1)}, bf16[96,3,384]{2,0,1:T(8,128)(2,1)S(1)}, u32[]{:S(2)}, u32[]{:S(2)}) collective-permute-start(bf16[96,3,384]{2,0,1:T(8,128)(2,1)S(1)} %copy.50), channel_id=1, source_target_pairs={{1,0},{2,1},{3,2},{4,3},{5,4},{6,5},{7,6},{8,7},{9,8},{10,9},{11,1... | collective-permute-start | bytes 663560 | tf_op jit(solution)/shard_map/ppermute | solution.py:18
  98.5 6.0 %collective-permute-done.4 = bf16[96,3,384]{2,0,1:T(8,128)(2,1)S(1)} collective-permute-done((bf16[96,3,384]{2,0,1:T(8,128)(2,1)S(1)}, bf16[96,3,384]{2,0,1:T(8,128)(2,1)S(1)}, u32[]{:S(2)}, u32[]{:S(2)}) %collective-permute-start.4) | collective-permute-done | bytes 221216 | tf_op jit(solution)/shard_map/ppermute | solution.py:17
  105.0 3.9 %collective-permute-start.6 = (bf16[3,38,384]{2,1,0:T(8,128)(2,1)S(1)}, bf16[3,38,384]{2,1,0:T(8,128)(2,1)S(1)}, u32[]{:S(2)}, u32[]{:S(2)}) collective-permute-start(bf16[3,38,384]{2,1,0:T(8,128)(2,1)S(1)} %get-tuple-element.126), channel_id=1, source_target_pairs={{0,32},{32,64},{64,96},{1,33},{33,65},{65,97},{2,34},{34,66},{66,9... | collective-permute-start | bytes 262664 | tf_op jit(solution)/shard_map/ppermute | solution.py:17
  111.1 5.2 %collective-permute-done.7 = bf16[3,38,384]{2,1,0:T(8,128)(2,1)S(1)} collective-permute-done((bf16[3,38,384]{2,1,0:T(8,128)(2,1)S(1)}, bf16[3,38,384]{2,1,0:T(8,128)(2,1)S(1)}, u32[]{:S(2)}, u32[]{:S(2)}) %collective-permute-start.7) | collective-permute-done | bytes 87584 | tf_op jit(solution)/shard_map/ppermute | solution.py:18
  116.3 3.4 maximum_maximum_fusion.1
  120.1 36.1 %fusion.122 = (f32[96,32]{1,0:T(8,128)S(1)}, f32[96,32,384]{2,1,0:T(8,128)S(1)}) fusion(f32[384]{0:T(512)S(1)} %copy-done.41, f32[384]{0:T(512)S(1)} %copy-done.23, bf16[99,38,384]{2,1,0:T(8,128)(2,1)S(1)} %get-tuple-element.125, f32[384]{0:T(512)S(1)} %copy-done.24, f32[384]{0:T(512)S(1)} %copy-done.25, f32[384]{0:T(512)S(1)} %copy-done.26, ...), kind=kLoop, calls=%fused_computation.296 | loop fusion | flops 195818496 | bytes 106699776 | tf_op jit(solution)/shard_map/reduce_sum | solution.py:46
  159.2 9.3 %convolution_add_fusion = f32[3072,384]{1,0:T(8,128)} fusion(f32[384]{0:T(512)S(1)} %copy-done.56, bf16[3072,384]{1,0:T(8,128)(2,1)} %bitcast.77, f32[768]{0:T(1024)S(1)} %copy-done.54, bf16[2,768,384]{2,1,0:T(8,128)(2,1)} %param.21, bf16[2,384,768]{2,1,0:T(8,128)(2,1)} %param.19), kind=kOutput, calls=%fused_computation.85 | convolution fusion | flops 3648651264 | bytes 8262144 | tf_op jit(solution)/shard_map/dot_general | solution.py:54
  168.6 3.0 fusion.68
  172.0 2.6 fusion.81
  180.3 3.4 collective-permute-done.9
  184.1 2.8 fusion.126
  188.3 3.1 slice_bitcast_fusion
  191.3 4.3 %fusion.71 = f32[3072,1,192]{0,2,1:T(8,128)} fusion(bf16[3072,384]{1,0:T(8,128)(2,1)} %bitcast.74, f32[3072,384]{0,1:T(8,128)S(1)} %fusion.105, f32[3072,384]{0,1:T(8,128)S(1)} %fusion.101, f32[3072,768]{0,1:T(8,128)S(1)} %fusion.81, bf16[3,3,384,192]{2,3,1,0:T(8,128)(2,1)} %param.24), kind=kOutput, calls=%fused_computation.94 | convolution fusion | flops 454754304 | bytes 11943936 | tf_op jit(solution)/shard_map/dot_general | solution.py:82
  195.6 2.7 pad_maximum_fusion.1
  198.4 10.0 %copy.58 = f32[3072,2,192]{2,1,0:T(2,128)} copy(f32[3072,2,192]{0,2,1:T(8,128)} %pad_maximum_fusion.1) | data formatting | bytes 9437184 | tf_op jit(solution)/shard_map/stack | solution.py:89
  208.4 8.7 %stack_reshape.6 = f32[96,1,64,192]{3,2,0,1:T(8,128)} reshape(f32[3072,2,192]{2,1,0:T(2,128)} %copy.58) | data formatting | bytes 9437184 | tf_op jit(solution)/shard_map/stack;reshape | solution.py:95
  217.0 4.2 %pad_maximum_fusion.2 = f32[3072,2,192]{0,2,1:T(8,128)} fusion(f32[3072,1,192]{0,2,1:T(8,128)} %fusion.71, f32[3072,1,192]{0,2,1:T(8,128)S(1)} %copy-done.3), kind=kLoop, calls=%fused_computation.78 | loop fusion | flops 1179648 | bytes 9437184 | tf_op jit(solution)/shard_map/stack | solution.py:92
  221.3 9.8 %copy.59 = f32[3072,2,192]{2,1,0:T(2,128)} copy(f32[3072,2,192]{0,2,1:T(8,128)} %pad_maximum_fusion.2) | data formatting | bytes 9437184 | tf_op jit(solution)/shard_map/stack | solution.py:92
  231.1 8.5 %stack_reshape.7 = f32[96,1,64,192]{3,2,0,1:T(8,128)} reshape(f32[3072,2,192]{2,1,0:T(2,128)} %copy.59) | data formatting | bytes 9437184 | tf_op jit(solution)/shard_map/stack;reshape | solution.py:95
  239.5 11.6 %pad_maximum_fusion = f32[96,2,64,192]{3,2,0,1:T(8,128)} fusion(f32[96,1,64,192]{3,2,0,1:T(8,128)} %stack_reshape.7, f32[96,1,64,192]{3,2,0,1:T(8,128)} %stack_reshape.6), kind=kLoop, calls=%fused_computation.2 | loop fusion | flops 2359296 | bytes 18874368 | tf_op jit(solution)/shard_map/stack | solution.py:95
  251.1 11.2 %copy.60 = f32[96,2,64,192]{3,2,1,0:T(8,128)} copy(f32[96,2,64,192]{3,2,0,1:T(8,128)} %pad_maximum_fusion) | data formatting | bytes 18874368 | tf_op jit(solution)/shard_map/stack | solution.py:95
  262.4 6.5 %fusion = bf16[192,64,192]{2,1,0:T(8,128)(2,1)S(1)} fusion(f32[96,2,64,192]{3,2,1,0:T(8,128)} %copy.60, f32[192]{0:T(256)S(1)} %copy-done.58), kind=kLoop, calls=%fused_computation.4 | loop fusion | flops 4718592 | bytes 14156544 | tf_op jit(solution)/shard_map/convert_element_type | solution.py:98
  268.9 76.8 %all_to_all.18 = bf16[192,64,192]{2,1,0:T(8,128)(2,1)S(1)} all-to-all(bf16[192,64,192]{2,1,0:T(8,128)(2,1)S(1)} %fusion), channel_id=1, replica_groups=mesh['lat'=4,'lon'=32] {'lon'}, dimensions={0} | all-to-all | bytes 9437184 | tf_op jit(solution)/shard_map/all_to_all | solution.py:146
  345.6 3.2 copy.61
  348.8 8.0 %copy.62 = bf16[6,2048,192]{1,2,0:T(8,128)(2,1)} copy(bf16[6,2048,192]{2,1,0:T(8,128)(2,1)} %bitcast.71) | data formatting | bytes 9437184 | tf_op jit(solution)/shard_map/all_to_all | solution.py:146
  (176 shorter events, 37.2 us)
Async XLA Ops:
  0.0 19.1 %copy-start = (bf16[96,32,384]{2,1,0:T(8,128)(2,1)S(1)}, bf16[96,32,384]{2,1,0:T(8,128)(2,1)}, u32[]{:S(2)}) copy-start(bf16[96,32,384]{2,1,0:T(8,128)(2,1)} %param.13) | copy-start | bytes 7077892
  1.7 18.8 %collective-permute-start.1 = (bf16[96,3,384]{2,0,1:T(8,128)(2,1)S(1)}, bf16[96,3,384]{2,0,1:T(8,128)(2,1)S(1)}, u32[]{:S(2)}, u32[]{:S(2)}) collective-permute-start(bf16[96,3,384]{2,0,1:T(8,128)(2,1)S(1)} %copy.64), channel_id=1, source_target_pairs={{1,0},{2,1},{3,2},{4,3},{5,4},{6,5},{7,6},{8,7},{9,8},{10,9},{11,1... | collective-permute-start | bytes 663560 | tf_op jit(solution)/shard_map/ppermute | solution.py:18
  8.9 10.5 %collective-permute-start = (bf16[96,3,384]{2,0,1:T(8,128)(2,1)S(1)}, bf16[96,3,384]{2,0,1:T(8,128)(2,1)}, u32[]{:S(2)}, u32[]{:S(2)}) collective-permute-start(bf16[96,3,384]{2,0,1:T(8,128)(2,1)S(1)} %copy.63), channel_id=1, source_target_pairs={{0,1},{1,2},{2,3},{3,4},{4,5},{5,6},{6,7},{7,8},{8,9},{9,10},{10,1... | collective-permute-start | bytes 663560 | tf_op jit(solution)/shard_map/ppermute | solution.py:17
  20.9 17.7 %copy-start.44 = (f32[384]{0:T(512)S(1)}, f32[384]{0:T(512)}, u32[]{:S(2)}) copy-start(f32[384]{0:T(512)} %get-tuple-element.67) | copy-start | bytes 4612
  20.9 17.7 %copy-start.45 = (f32[384]{0:T(512)S(1)}, f32[384]{0:T(512)}, u32[]{:S(2)}) copy-start(f32[384]{0:T(512)} %get-tuple-element.68) | copy-start | bytes 4612
  20.9 17.7 %copy-start.46 = (f32[384]{0:T(512)S(1)}, f32[384]{0:T(512)}, u32[]{:S(2)}) copy-start(f32[384]{0:T(512)} %get-tuple-element.69) | copy-start | bytes 4612
  20.9 17.7 %copy-start.47 = (f32[384]{0:T(512)S(1)}, f32[384]{0:T(512)}, u32[]{:S(2)}) copy-start(f32[384]{0:T(512)} %get-tuple-element.70) | copy-start | bytes 4612
  20.9 17.7 %copy-start.48 = (f32[384]{0:T(512)S(1)}, f32[384]{0:T(512)}, u32[]{:S(2)}) copy-start(f32[384]{0:T(512)} %get-tuple-element.71) | copy-start | bytes 4612
  20.9 17.7 %copy-start.49 = (f32[384]{0:T(512)S(1)}, f32[384]{0:T(512)}, u32[]{:S(2)}) copy-start(f32[384]{0:T(512)} %get-tuple-element.72) | copy-start | bytes 4612
  21.0 17.7 %copy-start.50 = (f32[384]{0:T(512)S(1)}, f32[384]{0:T(512)}, u32[]{:S(2)}) copy-start(f32[384]{0:T(512)} %get-tuple-element.112) | copy-start | bytes 4612
  21.0 10.7 %collective-permute-start.2 = (bf16[3,38,384]{2,1,0:T(8,128)(2,1)S(1)}, bf16[3,38,384]{2,1,0:T(8,128)(2,1)S(1)}, u32[]{:S(2)}, u32[]{:S(2)}) collective-permute-start(bf16[3,38,384]{2,1,0:T(8,128)(2,1)S(1)} %get-tuple-element.130), channel_id=1, source_target_pairs={{0,32},{32,64},{64,96},{1,33},{33,65},{65,97},{2,34},{34,66},{66,9... | collective-permute-start | bytes 262664 | tf_op jit(solution)/shard_map/ppermute | solution.py:17
  27.8 7.4 %collective-permute-start.3 = (bf16[3,38,384]{2,1,0:T(8,128)(2,1)S(1)}, bf16[3,38,384]{2,1,0:T(8,128)(2,1)S(1)}, u32[]{:S(2)}, u32[]{:S(2)}) collective-permute-start(bf16[3,38,384]{2,1,0:T(8,128)(2,1)S(1)} %get-tuple-element.131), channel_id=1, source_target_pairs={{32,0},{64,32},{96,64},{33,1},{65,33},{97,65},{34,2},{66,34},{98,6... | collective-permute-start | bytes 262664 | tf_op jit(solution)/shard_map/ppermute | solution.py:18
  90.5 29.2 %copy-start.1 = (bf16[96,32,384]{2,1,0:T(8,128)(2,1)}, bf16[96,32,384]{2,1,0:T(8,128)(2,1)S(1)}, u32[]{:S(2)}) copy-start(bf16[96,32,384]{2,1,0:T(8,128)(2,1)S(1)} %fusion.42) | copy-start | bytes 7077892
  90.8 7.5 %collective-permute-start.5 = (bf16[96,3,384]{2,0,1:T(8,128)(2,1)S(1)}, bf16[96,3,384]{2,0,1:T(8,128)(2,1)S(1)}, u32[]{:S(2)}, u32[]{:S(2)}) collective-permute-start(bf16[96,3,384]{2,0,1:T(8,128)(2,1)S(1)} %copy.50), channel_id=1, source_target_pairs={{1,0},{2,1},{3,2},{4,3},{5,4},{6,5},{7,6},{8,7},{9,8},{10,9},{11,1... | collective-permute-start | bytes 663560 | tf_op jit(solution)/shard_map/ppermute | solution.py:18
  95.5 9.0 %collective-permute-start.4 = (bf16[96,3,384]{2,0,1:T(8,128)(2,1)S(1)}, bf16[96,3,384]{2,0,1:T(8,128)(2,1)S(1)}, u32[]{:S(2)}, u32[]{:S(2)}) collective-permute-start(bf16[96,3,384]{2,0,1:T(8,128)(2,1)S(1)} %copy.49), channel_id=1, source_target_pairs={{0,1},{1,2},{2,3},{3,4},{4,5},{5,6},{6,7},{7,8},{8,9},{9,10},{10,1... | collective-permute-start | bytes 663560 | tf_op jit(solution)/shard_map/ppermute | solution.py:17
  104.7 15.0 %copy-start.8 = (f32[384]{0:T(512)S(1)}, f32[384]{0:T(512)}, u32[]{:S(2)}) copy-start(f32[384]{0:T(512)} %get-tuple-element.29) | copy-start | bytes 4612
  104.7 15.0 %copy-start.9 = (f32[384]{0:T(512)S(1)}, f32[384]{0:T(512)}, u32[]{:S(2)}) copy-start(f32[384]{0:T(512)} %get-tuple-element.30) | copy-start | bytes 4612
  104.7 15.0 %copy-start.10 = (f32[384]{0:T(512)S(1)}, f32[384]{0:T(512)}, u32[]{:S(2)}) copy-start(f32[384]{0:T(512)} %get-tuple-element.31) | copy-start | bytes 4612
  104.7 15.0 %copy-start.11 = (f32[384]{0:T(512)S(1)}, f32[384]{0:T(512)}, u32[]{:S(2)}) copy-start(f32[384]{0:T(512)} %get-tuple-element.32) | copy-start | bytes 4612
  104.7 15.0 %copy-start.12 = (f32[384]{0:T(512)S(1)}, f32[384]{0:T(512)}, u32[]{:S(2)}) copy-start(f32[384]{0:T(512)} %get-tuple-element.33) | copy-start | bytes 4612
  104.8 15.0 %copy-start.13 = (f32[384]{0:T(512)S(1)}, f32[384]{0:T(512)}, u32[]{:S(2)}) copy-start(f32[384]{0:T(512)} %get-tuple-element.34) | copy-start | bytes 4612
  104.8 15.0 %copy-start.14 = (f32[384]{0:T(512)S(1)}, f32[384]{0:T(512)}, u32[]{:S(2)}) copy-start(f32[384]{0:T(512)} %get-tuple-element.35) | copy-start | bytes 4612
  104.8 15.0 %copy-start.15 = (f32[384]{0:T(512)S(1)}, f32[384]{0:T(512)}, u32[]{:S(2)}) copy-start(f32[384]{0:T(512)} %get-tuple-element.36) | copy-start | bytes 4612
  104.8 15.0 %copy-start.16 = (f32[384]{0:T(512)S(1)}, f32[384]{0:T(512)}, u32[]{:S(2)}) copy-start(f32[384]{0:T(512)} %get-tuple-element.37) | copy-start | bytes 4612
  104.8 15.0 %copy-start.17 = (f32[384]{0:T(512)S(1)}, f32[384]{0:T(512)}, u32[]{:S(2)}) copy-start(f32[384]{0:T(512)} %get-tuple-element.38) | copy-start | bytes 4612
  104.8 15.0 %copy-start.18 = (f32[384]{0:T(512)S(1)}, f32[384]{0:T(512)}, u32[]{:S(2)}) copy-start(f32[384]{0:T(512)} %get-tuple-element.39) | copy-start | bytes 4612
  104.8 15.0 %copy-start.19 = (f32[384]{0:T(512)S(1)}, f32[384]{0:T(512)}, u32[]{:S(2)}) copy-start(f32[384]{0:T(512)} %get-tuple-element.40) | copy-start | bytes 4612
  104.8 15.0 %copy-start.20 = (f32[384]{0:T(512)S(1)}, f32[384]{0:T(512)}, u32[]{:S(2)}) copy-start(f32[384]{0:T(512)} %get-tuple-element.41) | copy-start | bytes 4612
  105.0 6.0 %collective-permute-start.6 = (bf16[3,38,384]{2,1,0:T(8,128)(2,1)S(1)}, bf16[3,38,384]{2,1,0:T(8,128)(2,1)S(1)}, u32[]{:S(2)}, u32[]{:S(2)}) collective-permute-start(bf16[3,38,384]{2,1,0:T(8,128)(2,1)S(1)} %get-tuple-element.126), channel_id=1, source_target_pairs={{0,32},{32,64},{64,96},{1,33},{33,65},{65,97},{2,34},{34,66},{66,9... | collective-permute-start | bytes 262664 | tf_op jit(solution)/shard_map/ppermute | solution.py:17
  108.9 7.4 %collective-permute-start.7 = (bf16[3,38,384]{2,1,0:T(8,128)(2,1)S(1)}, bf16[3,38,384]{2,1,0:T(8,128)(2,1)S(1)}, u32[]{:S(2)}, u32[]{:S(2)}) collective-permute-start(bf16[3,38,384]{2,1,0:T(8,128)(2,1)S(1)} %get-tuple-element.127), channel_id=1, source_target_pairs={{32,0},{64,32},{96,64},{33,1},{65,33},{97,65},{34,2},{66,34},{98,6... | collective-permute-start | bytes 262664 | tf_op jit(solution)/shard_map/ppermute | solution.py:18
  171.7 3.5 collective-permute-start.8
  176.9 6.7 %collective-permute-start.9 = (bf16[1,33,384]{2,1,0:T(8,128)(2,1)S(1)}, bf16[1,33,384]{2,1,0:T(8,128)(2,1)S(1)}, u32[]{:S(2)}, u32[]{:S(2)}) collective-permute-start(bf16[1,33,384]{2,1,0:T(8,128)(2,1)S(1)} %pad_maximum_fusion.15), channel_id=1, source_target_pairs={{32,0},{64,32},{96,64},{33,1},{65,33},{97,65},{34,2},{66,34},{98,6... | collective-permute-start | bytes 76040 | tf_op jit(solution)/shard_map/ppermute | solution.py:32
  (37 other events, 403.2 us)
where the time goes:
time: 361 us; the launch traced here: 357 us
  other arithmetic  123 us (34%)
  local copies, waits for them, and re-layouts  78.3 us (22%)
  blocking collectives  76.8 us (21%)
  starting transfers between devices  29.3 us (8%)
  matrix products  28.2 us (8%)
  waiting for transfers between devices  20.7 us (6%)
    all_to_all x1, blocking collectives, local(): lax.all_to_all(local_fine, 'lon', split_axis=0, concat_axis=1, tiled=True)  76.8 us
    reduce_sum x2, other arithmetic, mixer(): center = jnp.mean(depth, -1, keepdims=True)  72.6 us
    another operation x3, local copies, waits for them, and re-layouts, upsample(): jnp.stack([upper_rows, bottom_rows], 1)  28.4 us
    dot_general x2, matrix products, mixer(): jnp.dot(hidden, out_weight, preferred_element_type=jnp.float32) + out_bias  18.4 us
    ppermute x4, starting transfers between devices, padded_2(): after = lax.ppermute(initial, axis, down)  16.4 us
    another operation x1, other arithmetic, upsample(): jnp.stack([upper_rows, bottom_rows], 1)  11.6 us
    all_to_all x2, local copies, waits for them, and re-layouts, local(): lax.all_to_all(local_fine, 'lon', split_axis=0, concat_axis=1, tiled=True)  11.3 us
    ppermute x4, waiting for transfers between devices, padded_2(): after = lax.ppermute(initial, axis, down)  10.8 us
  transfers between devices with their start and end apart: 10, of which 6 were waited for; matrix products, arithmetic and copies ran while one was open for 5% of the time, Pallas kernels for 0%

commit v1 on v0

v1 whole, which is shorter than its diff:
```python
import functools
import jax
import jax.numpy as jnp
from jax import lax
from jax.experimental import pallas as pl
from jax.experimental.pallas import tpu as pltpu

TS = 32
R = 8
COL0 = 8


def depthwise_block(x_ref, wb_ref, bias, d_ref, row0, groups):
    for g in range(groups):
        for cb in range(4):
            total = jnp.zeros((R, 8, 128), jnp.float32)
            for b in range(7):
                start = COL0 - 3 + b + 8 * cb
                window = x_ref[g, pl.ds(row0, R + 6), start : start + 8, :]
                for a in range(7):
                    total = total + window[a : a + R] * wb_ref[a * 7 + b, g]
            d_ref[:, 8 * cb : 8 * cb + 8, 128 * g : 128 * g + 128] = (
                total + bias[:, 128 * g : 128 * g + 128]
            )


def mix_block(depth, gain, shift, w_in, b_in, w_out, b_out):
    center = jnp.mean(depth, -1, keepdims=True)
    offset = depth - center
    spread = jnp.mean(offset * offset, -1, keepdims=True)
    normed = (offset * lax.rsqrt(spread + 1e-06) * gain + shift).astype(jnp.bfloat16)
    hidden = jnp.dot(normed, w_in, preferred_element_type=jnp.float32) + b_in
    inner = hidden * (0.7978845608028654 + 0.035677408136300125 * (hidden * hidden))
    half = 0.5 * hidden
    hidden = (half + half * jnp.tanh(inner)).astype(jnp.bfloat16)
    return jnp.dot(hidden, w_out, preferred_element_type=jnp.float32) + b_out


def layer_kernel(tiles_ref, pad_ref, dw_ref, dwb_ref, gain_ref, shift_ref, win_ref, bin_ref,
                 wout_ref, bout_ref, scale_ref, out_ref, x_ref, wb_ref, d_ref):
    height, width, channels = out_ref.shape
    groups = channels // 128
    for k in range(49):
        for g in range(groups):
            wb_ref[k, g] = jnp.broadcast_to(dw_ref[k : k + 1, 128 * g : 128 * g + 128], (8, 128))

    @pl.loop(0, (height + 6) // 6)
    def _(i):
        rows = pl.ds(i * 6, 6)
        for g in range(groups):
            x_ref[g, rows] = pad_ref[rows, :, 128 * g : 128 * g + 128].astype(jnp.float32)

    blocks = TS // R
    m0, m1, m2 = tiles_ref[0, 0], tiles_ref[1, 0], tiles_ref[2, 0]
    for t in range(3):
        @pl.when(tiles_ref[t, 0] == 0)
        def _():
            out_ref[TS * t : TS * t + TS] = pad_ref[3 + TS * t : 3 + TS * t + TS, COL0 : COL0 + width]

        @pl.when(tiles_ref[t, 0] != 0)
        def _():
            @pl.loop(0, blocks)
            def _(i):
                row0 = t * TS + i * R
                depthwise_block(x_ref, wb_ref, dwb_ref[...], d_ref, row0, groups)
                update = mix_block(d_ref[...].reshape(R * width, channels), gain_ref[...], shift_ref[...],
                                   win_ref[...], bin_ref[...], wout_ref[...], bout_ref[...])
                field = pad_ref[pl.ds(3 + row0, R), COL0 : COL0 + width].astype(jnp.float32)
                mask = tiles_ref[t, 0].astype(jnp.float32)
                out_ref[pl.ds(row0, R)] = (
                    field + (mask * scale_ref[...]) * update.reshape(R, width, channels)
                ).astype(jnp.bfloat16)


def layer_call(tiles, padded, *params):
    height, width, channels = padded.shape[0] - 6, padded.shape[1] - 16, padded.shape[2]
    vmem = pl.BlockSpec(memory_space=pltpu.VMEM)
    return pl.pallas_call(
        layer_kernel,
        out_shape=jax.ShapeDtypeStruct((height, width, channels), jnp.bfloat16),
        in_specs=[pl.BlockSpec(memory_space=pltpu.SMEM)] + [vmem] * (1 + len(params)),
        out_specs=vmem,
        scratch_shapes=[
            pltpu.VMEM((channels // 128, height + 6, width + 16, 128), jnp.float32),
            pltpu.VMEM((49, channels // 128, 8, 128), jnp.float32),
            pltpu.VMEM((R, width, channels), jnp.float32),
        ],
        compiler_params=pltpu.CompilerParams(vmem_limit_bytes=48 * 1024 * 1024),
    )(tiles, padded, *params)


UCH = 256


def upsample_kernel(y_ref, next_ref, w_ee, w_eo, w_oe, w_oo, bias_ref, out_ref, f_ref):
    width_out = out_ref.shape[2]
    wides = []
    for i in range(4):
        cur = y_ref[i]
        both = jnp.concatenate([cur, next_ref[i]], 0).astype(jnp.float32)
        right = both[1 : 1 + UCH].astype(jnp.bfloat16)
        wides.append((cur, right))
    bias = bias_ref[...]
    for i in range(3):
        cur, right = wides[i]
        low, corner = wides[i + 1]
        ee = jnp.dot(cur, w_ee[...], preferred_element_type=jnp.float32) + bias
        eo = jnp.dot(jnp.concatenate([cur, right], 1), w_eo[...], preferred_element_type=jnp.float32) + bias
        oe = jnp.dot(jnp.concatenate([cur, low], 1), w_oe[...], preferred_element_type=jnp.float32) + bias
        oo = jnp.dot(jnp.concatenate([cur, right, low, corner], 1), w_oo[...], preferred_element_type=jnp.float32) + bias
        for p, (even, odd) in enumerate(((ee, eo), (oe, oo))):
            for k, lanes in enumerate((slice(0, 128), slice(128, width_out))):
                wide = lanes.stop - lanes.start
                f_ref[k, pl.ds(0, UCH, stride=2), :wide] = even[:, lanes]
                f_ref[k, pl.ds(1, UCH, stride=2), :wide] = odd[:, lanes]
                out_ref[2 * i + p, :, lanes] = f_ref[k, :, :wide].astype(jnp.bfloat16)


def upsample_call(y, weight, bias):
    rows, width, channels = y.shape
    out_width = weight.shape[3]
    w_ee = weight[1, 1]
    w_eo = jnp.concatenate([weight[1, 2], weight[1, 0]], 0)
    w_oe = jnp.concatenate([weight[2, 1], weight[0, 1]], 0)
    w_oo = jnp.concatenate([weight[2, 2], weight[2, 0], weight[0, 2], weight[0, 0]], 0)
    chunks = width // UCH
    whole = lambda w: pl.BlockSpec(w.shape, lambda j: (0,) * w.ndim)
    bias = bias.reshape(1, -1)
    return pl.pallas_call(
        upsample_kernel,
        grid=(chunks,),
        out_shape=jax.ShapeDtypeStruct((2 * rows - 2, 2 * width, out_width), jnp.bfloat16),
        in_specs=[
            pl.BlockSpec((rows, UCH, channels), lambda j: (0, j, 0)),
            pl.BlockSpec((rows, 16, channels), lambda j: (0, ((j + 1) % chunks) * (UCH // 16), 0)),
            whole(w_ee), whole(w_eo), whole(w_oe), whole(w_oo), whole(bias),
        ],
        out_specs=pl.BlockSpec((2 * rows - 2, 2 * UCH, out_width), lambda j: (0, j, 0)),
        scratch_shapes=[pltpu.VMEM((2, 2 * UCH, 128), jnp.float32)],
        compiler_params=pltpu.CompilerParams(vmem_limit_bytes=48 * 1024 * 1024),
    )(y, y, w_ee, w_eo, w_oe, w_oo, bias)


def local(coarse, ocean_tiles, dw_weight, dw_bias, norm_gain, norm_shift, in_weight, in_bias,
          out_weight, out_bias, layer_scale, up_weight, up_bias):
    height, width, channels = coarse.shape
    size = lax.axis_size("lon")
    up = [(i, (i + 1) % size) for i in range(size)]
    down = [(j, i) for i, j in up]
    lat_up = [(i, i + 1) for i in range(lax.axis_size("lat") - 1)]
    lat_down = [(j, i) for i, j in lat_up]
    field = coarse
    for l in range(2):
        before = lax.ppermute(field[:, -3:], "lon", up)
        after = lax.ppermute(field[:, :3], "lon", down)
        wide = jnp.concatenate([before, field, after], 1)
        above = lax.ppermute(wide[-3:], "lat", lat_up)
        below = lax.ppermute(wide[:3], "lat", lat_down)
        padded = jnp.pad(jnp.concatenate([above, wide, below], 0), ((0, 0), (5, 5), (0, 0)))
        row = lambda v: v[l].reshape(1, -1)
        field = layer_call(ocean_tiles, padded, dw_weight[l].reshape(49, channels), row(dw_bias),
                           row(norm_gain), row(norm_shift), in_weight[l], row(in_bias),
                           out_weight[l], row(out_bias), row(layer_scale))
    below = lax.ppermute(field[:1], "lat", lat_down)
    owned = field.reshape(size, height // size, width, channels)
    last = jnp.concatenate([owned[1:, :1], below[None]], 0)
    sent = jnp.concatenate([owned, last], 1)
    got = lax.all_to_all(sent, "lon", split_axis=0, concat_axis=0, tiled=True)
    rows = got.transpose(1, 0, 2, 3).reshape(height // size + 1, size * width, channels)
    return upsample_call(rows, up_weight, up_bias)


def solution(mesh):
    from jax.sharding import PartitionSpec as P
    placed = (P("lat", "lon", None), P("lat", "lon")) + (P(),) * 11
    return jax.shard_map(
        local, mesh=mesh, in_specs=placed, out_specs=P(("lat", "lon"), None, None), check_vma=False
    )
```

time: 361 us -> 205 us (0.57)
  other arithmetic: 123 us -> 16.1 us
  blocking collectives: 76.8 us -> 0 us
  Pallas kernels: 0 us -> 60.4 us
  local copies, waits for them, and re-layouts: 78.3 us -> 33.8 us
  waiting for transfers between devices: 20.7 us -> 57.2 us
  matrix products: 28.2 us -> 0 us
  starting transfers between devices: 29.3 us -> 35.9 us
    all_to_all x1 -> x0, blocking collectives: 76.8 us -> none  [local(): lax.all_to_all(local_fine, 'lon', split_axis=0, concat_axis=1, tiled=True)]
    reduce_sum x4 -> x0, other arithmetic: 74.4 us -> none  [the longest x2 72.6 us: mixer(): center = jnp.mean(depth, -1, keepdims=True)]
    pallas_call x0 -> x3, Pallas kernels: none -> 60.4 us  [the longest x2 51.5 us: layer_call(): pl.pallas_call(layer_kernel, out_shape=jax.ShapeDtypeStruct((height, widt...]
    another operation x5 -> x2, local copies, waits for them, and re-layouts: 48.1 us -> 3.04 us  [local(): dw_weight[l].reshape(49, channels)]
    all_to_all x0 -> x1, waiting for transfers between devices: none -> 36.6 us  [local(): got = lax.all_to_all(sent, 'lon', split_axis=0, concat_axis=0, tiled=True)]
    dot_general x6 -> x0, matrix products: 28.2 us -> none  [the longest x2 18.4 us: mixer(): jnp.dot(hidden, out_weight, preferred_element_type=jnp.float32) + out_bias]
    another operation x4 -> x0, other arithmetic: 21.7 us -> none  [the longest x1 11.6 us: upsample(): jnp.stack([upper_rows, bottom_rows], 1)]
    convert_element_type x5 -> x0, other arithmetic: 16.7 us -> none  [the longest x1 6.47 us: upsample(): return (whole + bias).astype(jnp.bfloat16)]
  transfers between devices with their start and end apart: 10 -> 10, of which waited for: 6 -> 7; matrix products, arithmetic and copies ran while one was open for 5% -> 7% of each run, Pallas kernels for 0% -> 0%
where the time goes in v1:
time: 205 us; the launch traced here: 204 us
  Pallas kernels  60.4 us (29%)
  waiting for transfers between devices  57.2 us (28%)
  starting transfers between devices  35.9 us (18%)
  local copies, waits for them, and re-layouts  33.8 us (16%)
  other arithmetic  16.1 us (8%)
    pallas_call x2, Pallas kernels, layer_call(): pl.pallas_call(layer_kernel, out_shape=jax.ShapeDtypeStruct((height, widt...  51.5 us
    all_to_all x1, waiting for transfers between devices, local(): got = lax.all_to_all(sent, 'lon', split_axis=0, concat_axis=0, tiled=True)  36.6 us
    concatenate x2, other arithmetic, local(): jnp.concatenate([above, wide, below], 0)  11.7 us
    ppermute x2, starting transfers between devices, local(): after = lax.ppermute(field[:, :3], 'lon', down)  10.3 us
    ppermute x2, starting transfers between devices, local(): above = lax.ppermute(wide[-3:], 'lat', lat_up)  10.3 us
    unnamed x58, local copies, waits for them, and re-layouts  9.54 us
    pallas_call x1, Pallas kernels, upsample_call(): pl.pallas_call(upsample_kernel, grid=(chunks,), out_shape=jax.ShapeDtypeS...  8.95 us
    pallas_call x1, local copies, waits for them, and re-layouts, upsample_call(): pl.pallas_call(upsample_kernel, grid=(chunks,), out_shape=jax.ShapeDtypeS...  8.03 us
  transfers between devices with their start and end apart: 10, of which 7 were waited for; matrix products, arithmetic and copies ran while one was open for 7% of the time, Pallas kernels for 0%

profile of v1, /device:TPU:1, one launch (start us, length us, event | category | flops | bytes accessed | tf_op | source)
XLA Modules:
  0.0 203.7 jit_solution(5413247454832859059)
XLA Ops:
  0.0 2.4 %fusion.16 = (bf16[96,3,384]{2,1,0:T(4,128)(2,1)}, bf16[96,3,384]{2,1,0:T(4,128)(2,1)}) fusion(bf16[96,32,384]{2,1,0:T(8,128)(2,1)} %param.13), kind=kLoop, calls=%fused_computation.36 | loop fusion | bytes 884736 | tf_op jit(solution)/shard_map/slice | solution.py:154
  2.4 2.5 %collective-permute-start = (bf16[96,3,384]{2,1,0:T(4,128)(2,1)}, bf16[96,3,384]{2,1,0:T(4,128)(2,1)}, u32[]{:S(2)}, u32[]{:S(2)}) collective-permute-start(bf16[96,3,384]{2,1,0:T(4,128)(2,1)} %get-tuple-element.13), channel_id=1, source_target_pairs={{0,1},{1,2},{2,3},{3,4},{4,5},{5,6},{6,7},{7,8},{8,9},{9,10},{10,1... | collective-permute-start | bytes 663560 | tf_op jit(solution)/shard_map/ppermute | solution.py:154
  4.9 4.6 %collective-permute-start.1 = (bf16[96,3,384]{2,1,0:T(4,128)(2,1)}, bf16[96,3,384]{2,1,0:T(4,128)(2,1)}, u32[]{:S(2)}, u32[]{:S(2)}) collective-permute-start(bf16[96,3,384]{2,1,0:T(4,128)(2,1)} %get-tuple-element.14), channel_id=1, source_target_pairs={{1,0},{2,1},{3,2},{4,3},{5,4},{6,5},{7,6},{8,7},{9,8},{10,9},{11,1... | collective-permute-start | bytes 663560 | tf_op jit(solution)/shard_map/ppermute | solution.py:155
  11.1 2.2 %slice_bitcast_fusion.1 = (bf16[384,768]{1,0:T(8,128)(2,1)S(1)}, bf16[384,768]{1,0:T(8,128)(2,1)}) fusion(bf16[2,384,768]{2,1,0:T(8,128)(2,1)} %param.19), kind=kLoop, calls=%fused_computation.22 | loop fusion | bytes 2359296 | tf_op jit(solution)/shard_map/squeeze | solution.py:162
  13.3 2.2 %slice_bitcast_fusion = (bf16[768,384]{1,0:T(8,128)(2,1)S(1)}, bf16[768,384]{1,0:T(8,128)(2,1)}) fusion(bf16[2,768,384]{2,1,0:T(8,128)(2,1)} %param.21), kind=kLoop, calls=%fused_computation.21 | loop fusion | bytes 2359296 | tf_op jit(solution)/shard_map/squeeze | solution.py:163
  17.3 1.8 collective-permute-done.1
  19.1 1.5 pad_maximum_fusion.8
  20.6 7.0 %collective-permute-start.2 = (bf16[3,38,384]{2,1,0:T(8,128)(2,1)}, bf16[3,38,384]{2,1,0:T(8,128)(2,1)}, u32[]{:S(2)}, u32[]{:S(2)}) collective-permute-start(bf16[3,38,384]{2,1,0:T(8,128)(2,1)} %get-tuple-element.9), channel_id=1, source_target_pairs={{0,32},{32,64},{64,96},{1,33},{33,65},{65,97},{2,34},{34,66},{66,9... | collective-permute-start | bytes 262664 | tf_op jit(solution)/shard_map/ppermute | solution.py:157
  27.5 1.9 collective-permute-start.3
  30.5 1.5 reshape_squeeze.6.dw_ref
  32.0 3.2 %collective-permute-done.3 = bf16[3,38,384]{2,1,0:T(8,128)(2,1)} collective-permute-done((bf16[3,38,384]{2,1,0:T(8,128)(2,1)}, bf16[3,38,384]{2,1,0:T(8,128)(2,1)}, u32[]{:S(2)}, u32[]{:S(2)}) %collective-permute-start.3) | collective-permute-done | bytes 87584 | tf_op jit(solution)/shard_map/ppermute | solution.py:158
  35.2 5.8 %fusion.10.pad_ref = bf16[102,48,384]{2,1,0:T(8,128)(2,1)} fusion(bf16[3,38,384]{2,1,0:T(8,128)(2,1)} %collective-permute-done.3, bf16[3,38,384]{2,1,0:T(8,128)(2,1)} %collective-permute-done.2, bf16[96,3,384]{2,1,0:T(4,128)(2,1)} %collective-permute-done.1, bf16[96,32,384]{2,1,0:T(8,128)(2,1)S(1)} %copy-done.14, bf16[96,3,384]{2,1,0:T(4,128)(2,1)} %collective-permute-done), kind=kLoop, calls=%fused_computation.14 | loop fusion | flops 33841152 | bytes 6736896 | tf_op jit(solution)/shard_map/concatenate | solution.py:159
  41.1 1.1 copy-done
  42.1 1.1 copy-done.1
  46.5 25.7 %shard_map.127 = bf16[96,32,384]{2,1,0:T(8,128)(2,1)S(1)} custom-call(s32[3,1]{1,0:T(4,128)S(1)} %copy.45.tiles_ref, bf16[102,48,384]{2,1,0:T(8,128)(2,1)} %fusion.10.pad_ref, f32[49,384]{1,0:T(8,128)S(1)} %copy-done.3, f32[1,384]{1,0:T(1,128)S(1)} %copy-done.12, f32[1,384]{1,0:T(1,128)S(1)} %copy-done.8, f32[1,384]{1,0:T(1,128)S(1)} %copy-done.7, ...), custom_call_target="tpu_custom_call" | custom-call | tf_op jit(solution)/shard_map/pallas_call | solution.py:78
  72.5 5.7 %collective-permute-start.5 = (bf16[96,3,384]{2,1,0:T(4,128)(2,1)S(1)}, bf16[96,3,384]{2,1,0:T(4,128)(2,1)S(1)}, u32[]{:S(2)}, u32[]{:S(2)}) collective-permute-start(bf16[96,3,384]{2,1,0:T(4,128)(2,1)S(1)} %get-tuple-element.12), channel_id=1, source_target_pairs={{1,0},{2,1},{3,2},{4,3},{5,4},{6,5},{7,6},{8,7},{9,8},{10,9},{11,1... | collective-permute-start | bytes 663560 | tf_op jit(solution)/shard_map/ppermute | solution.py:155
  78.2 4.2 %collective-permute-done.4 = bf16[96,3,384]{2,1,0:T(4,128)(2,1)S(1)} collective-permute-done((bf16[96,3,384]{2,1,0:T(4,128)(2,1)S(1)}, bf16[96,3,384]{2,1,0:T(4,128)(2,1)S(1)}, u32[]{:S(2)}, u32[]{:S(2)}) %collective-permute-start.4) | collective-permute-done | bytes 221216 | tf_op jit(solution)/shard_map/ppermute | solution.py:154
  82.4 2.6 %collective-permute-done.5 = bf16[96,3,384]{2,1,0:T(4,128)(2,1)S(1)} collective-permute-done((bf16[96,3,384]{2,1,0:T(4,128)(2,1)S(1)}, bf16[96,3,384]{2,1,0:T(4,128)(2,1)S(1)}, u32[]{:S(2)}, u32[]{:S(2)}) %collective-permute-start.5) | collective-permute-done | bytes 221216 | tf_op jit(solution)/shard_map/ppermute | solution.py:155
  85.7 3.4 %collective-permute-start.6 = (bf16[3,38,384]{2,1,0:T(8,128)(2,1)}, bf16[3,38,384]{2,1,0:T(8,128)(2,1)}, u32[]{:S(2)}, u32[]{:S(2)}) collective-permute-start(bf16[3,38,384]{2,1,0:T(8,128)(2,1)} %get-tuple-element.7), channel_id=1, source_target_pairs={{0,32},{32,64},{64,96},{1,33},{33,65},{65,97},{2,34},{34,66},{66,9... | collective-permute-start | bytes 262664 | tf_op jit(solution)/shard_map/ppermute | solution.py:157
  89.1 1.9 collective-permute-start.7
  91.0 1.5 reshape_squeeze.7.dw_ref
  92.5 4.2 %collective-permute-done.7 = bf16[3,38,384]{2,1,0:T(8,128)(2,1)} collective-permute-done((bf16[3,38,384]{2,1,0:T(8,128)(2,1)}, bf16[3,38,384]{2,1,0:T(8,128)(2,1)}, u32[]{:S(2)}, u32[]{:S(2)}) %collective-permute-start.7) | collective-permute-done | bytes 87584 | tf_op jit(solution)/shard_map/ppermute | solution.py:158
  96.8 5.8 %select_maximum_fusion.pad_ref = bf16[102,48,384]{2,1,0:T(8,128)(2,1)} fusion(bf16[3,38,384]{2,1,0:T(8,128)(2,1)} %collective-permute-done.7, bf16[3,38,384]{2,1,0:T(8,128)(2,1)} %collective-permute-done.6, bf16[96,3,384]{2,1,0:T(4,128)(2,1)} %copy-done.17, bf16[96,32,384]{2,1,0:T(8,128)(2,1)S(1)} %shard_map.127, bf16[96,3,384]{2,1,0:T(4,128)(2,1)} %copy-done.16), kind=kLoop, calls=%fused_computation.3 | loop fusion | flops 33841152 | bytes 6736896 | tf_op jit(solution)/shard_map/concatenate | solution.py:159
  104.6 25.8 %shard_map.128 = bf16[96,32,384]{2,1,0:T(8,128)(2,1)S(1)} custom-call(s32[3,1]{1,0:T(4,128)S(1)} %copy.45.tiles_ref, bf16[102,48,384]{2,1,0:T(8,128)(2,1)} %select_maximum_fusion.pad_ref, f32[49,384]{1,0:T(8,128)S(1)} %copy-done.2, f32[1,384]{1,0:T(1,128)S(1)} %copy-done.11, f32[1,384]{1,0:T(1,128)S(1)} %copy-done.4, ...), custom_call_target="tpu_custom_call" | custom-call | tf_op jit(solution)/shard_map/pallas_call | solution.py:78
  130.5 1.9 collective-permute-start.8
  132.5 4.6 %collective-permute-done.8 = bf16[1,32,384]{2,1,0:T(8,128)(2,1)S(1)} collective-permute-done((bf16[1,32,384]{2,1,0:T(8,128)(2,1)S(1)}, bf16[1,32,384]{2,1,0:T(8,128)(2,1)S(1)}, u32[]{:S(2)}, u32[]{:S(2)}) %collective-permute-start.8) | collective-permute-done | bytes 24608 | tf_op jit(solution)/shard_map/ppermute | solution.py:164
  137.1 2.0 maximum_maximum_fusion
  139.1 7.0 %all-to-all-start = ((bf16[32,4,32,384]{3,2,1,0:T(8,128)(2,1)}), bf16[32,4,32,384]{3,2,1,0:T(8,128)(2,1)}, u32[]{:S(2)}, u32[]{:S(2)}) async-start(bf16[32,4,32,384]{3,2,1,0:T(8,128)(2,1)} %maximum_maximum_fusion), calls=%async_computation | async-start | bytes 6291456 | tf_op jit(solution)/shard_map/all_to_all | solution.py:168
  147.9 36.6 %all-to-all-done = bf16[32,4,32,384]{3,2,1,0:T(8,128)(2,1)} async-done(((bf16[32,4,32,384]{3,2,1,0:T(8,128)(2,1)}), bf16[32,4,32,384]{3,2,1,0:T(8,128)(2,1)}, u32[]{:S(2)}, u32[]{:S(2)}) %all-to-all-start) | async-done | bytes 3145760 | tf_op jit(solution)/shard_map/all_to_all | solution.py:168
  184.4 2.3 %copy.46 = bf16[4,32,32,384]{3,2,1,0:T(8,128)(2,1)S(1)} copy(bf16[4,32,32,384]{3,2,0,1:T(8,128)(2,1)} %bitcast.6) | data formatting | bytes 6291456 | tf_op jit(solution)/shard_map/transpose | solution.py:169
  186.8 8.9 %shard_map.129 = bf16[6,2048,192]{2,1,0:T(8,128)(2,1)} custom-call(bf16[4,1024,384]{2,1,0:T(8,128)(2,1)S(1)} %bitcast.22, bf16[4,1024,384]{2,1,0:T(8,128)(2,1)S(1)} %bitcast.23, bf16[384,192]{1,0:T(8,128)(2,1)S(1)} %bitcast.26, bf16[768,192]{1,0:T(8,128)(2,1)S(1)} %get-tuple-element.44.w_eo, bf16[768,192]{1,0:T(8,128)(2,1)S(1)} %get-tuple-element.45.w_oe, ...), custom_call_target="tpu_custom_call" | custom-call | tf_op jit(solution)/shard_map/pallas_call | solution.py:129
  195.7 8.0 %copy.56 = bf16[6,2048,192]{1,2,0:T(8,128)(2,1)} copy(bf16[6,2048,192]{2,1,0:T(8,128)(2,1)} %shard_map.129) | data formatting | bytes 9437184 | tf_op jit(solution)/shard_map/pallas_call | solution.py:129
  (72 shorter events, 12.6 us)
Async XLA Ops:
  0.0 19.1 %copy-start.14 = (bf16[96,32,384]{2,1,0:T(8,128)(2,1)S(1)}, bf16[96,32,384]{2,1,0:T(8,128)(2,1)}, u32[]{:S(2)}) copy-start(bf16[96,32,384]{2,1,0:T(8,128)(2,1)} %param.13) | copy-start | bytes 7077892
  2.4 14.9 %collective-permute-start = (bf16[96,3,384]{2,1,0:T(4,128)(2,1)}, bf16[96,3,384]{2,1,0:T(4,128)(2,1)}, u32[]{:S(2)}, u32[]{:S(2)}) collective-permute-start(bf16[96,3,384]{2,1,0:T(4,128)(2,1)} %get-tuple-element.13), channel_id=1, source_target_pairs={{0,1},{1,2},{2,3},{3,4},{4,5},{5,6},{6,7},{7,8},{8,9},{9,10},{10,1... | collective-permute-start | bytes 663560 | tf_op jit(solution)/shard_map/ppermute | solution.py:154
  4.9 14.2 %collective-permute-start.1 = (bf16[96,3,384]{2,1,0:T(4,128)(2,1)}, bf16[96,3,384]{2,1,0:T(4,128)(2,1)}, u32[]{:S(2)}, u32[]{:S(2)}) collective-permute-start(bf16[96,3,384]{2,1,0:T(4,128)(2,1)} %get-tuple-element.14), channel_id=1, source_target_pairs={{1,0},{2,1},{3,2},{4,3},{5,4},{6,5},{7,6},{8,7},{9,8},{10,9},{11,1... | collective-permute-start | bytes 663560 | tf_op jit(solution)/shard_map/ppermute | solution.py:155
  10.3 5.2 %copy-start.20 = (f32[2,384]{1,0:T(2,128)S(1)}, f32[2,384]{1,0:T(2,128)}, u32[]{:S(2)}) copy-start(f32[2,384]{1,0:T(2,128)} %param.18) | copy-start | bytes 9220
  10.3 5.2 %copy-start.21 = (f32[2,384]{1,0:T(2,128)S(1)}, f32[2,384]{1,0:T(2,128)}, u32[]{:S(2)}) copy-start(f32[2,384]{1,0:T(2,128)} %param.17) | copy-start | bytes 9220
  10.3 5.8 %copy-start.22 = (f32[2,384]{1,0:T(2,128)S(1)}, f32[2,384]{1,0:T(2,128)}, u32[]{:S(2)}) copy-start(f32[2,384]{1,0:T(2,128)} %param.23) | copy-start | bytes 9220
  10.3 5.8 %copy-start.23 = (f32[2,384]{1,0:T(2,128)S(1)}, f32[2,384]{1,0:T(2,128)}, u32[]{:S(2)}) copy-start(f32[2,384]{1,0:T(2,128)} %param.22) | copy-start | bytes 9220
  10.3 6.4 %copy-start.19 = (f32[2,384]{1,0:T(2,128)S(1)}, f32[2,384]{1,0:T(2,128)}, u32[]{:S(2)}) copy-start(f32[2,384]{1,0:T(2,128)} %param.16) | copy-start | bytes 9220
  11.1 18.4 %copy-start.18 = (f32[2,7,7,384]{3,0,2,1:T(2,128)S(1)}, f32[2,7,7,384]{3,0,2,1:T(2,128)}, u32[]{:S(2)}) copy-start(f32[2,7,7,384]{3,0,2,1:T(2,128)} %param.15) | copy-start | bytes 451588
  20.6 11.4 %collective-permute-start.2 = (bf16[3,38,384]{2,1,0:T(8,128)(2,1)}, bf16[3,38,384]{2,1,0:T(8,128)(2,1)}, u32[]{:S(2)}, u32[]{:S(2)}) collective-permute-start(bf16[3,38,384]{2,1,0:T(8,128)(2,1)} %get-tuple-element.9), channel_id=1, source_target_pairs={{0,32},{32,64},{64,96},{1,33},{33,65},{65,97},{2,34},{34,66},{66,9... | collective-permute-start | bytes 262664 | tf_op jit(solution)/shard_map/ppermute | solution.py:157
  27.5 7.7 %collective-permute-start.3 = (bf16[3,38,384]{2,1,0:T(8,128)(2,1)}, bf16[3,38,384]{2,1,0:T(8,128)(2,1)}, u32[]{:S(2)}, u32[]{:S(2)}) collective-permute-start(bf16[3,38,384]{2,1,0:T(8,128)(2,1)} %get-tuple-element.10), channel_id=1, source_target_pairs={{32,0},{64,32},{96,64},{33,1},{65,33},{97,65},{34,2},{66,34},{98,6... | collective-permute-start | bytes 262664 | tf_op jit(solution)/shard_map/ppermute | solution.py:158
  32.0 9.1 %copy-start.3 = (f32[49,384]{1,0:T(8,128)S(1)}, f32[49,384]{1,0:T(8,128)}, u32[]{:S(2)}) copy-start(f32[49,384]{1,0:T(8,128)} %reshape_squeeze.6.dw_ref) | copy-start | bytes 225796
  41.1 1.1 copy-start
  42.1 1.1 copy-start.1
  43.2 0.7 copy-start.7
  43.9 0.7 copy-start.8
  45.2 0.7 copy-start.10
  45.9 0.7 copy-start.12
  72.4 9.9 %collective-permute-start.4 = (bf16[96,3,384]{2,1,0:T(4,128)(2,1)S(1)}, bf16[96,3,384]{2,1,0:T(4,128)(2,1)S(1)}, u32[]{:S(2)}, u32[]{:S(2)}) collective-permute-start(bf16[96,3,384]{2,1,0:T(4,128)(2,1)S(1)} %get-tuple-element.11), channel_id=1, source_target_pairs={{0,1},{1,2},{2,3},{3,4},{4,5},{5,6},{6,7},{7,8},{8,9},{9,10},{10,1... | collective-permute-start | bytes 663560 | tf_op jit(solution)/shard_map/ppermute | solution.py:154
  72.5 12.4 %collective-permute-start.5 = (bf16[96,3,384]{2,1,0:T(4,128)(2,1)S(1)}, bf16[96,3,384]{2,1,0:T(4,128)(2,1)S(1)}, u32[]{:S(2)}, u32[]{:S(2)}) collective-permute-start(bf16[96,3,384]{2,1,0:T(4,128)(2,1)S(1)} %get-tuple-element.12), channel_id=1, source_target_pairs={{1,0},{2,1},{3,2},{4,3},{5,4},{6,5},{7,6},{8,7},{9,8},{10,9},{11,1... | collective-permute-start | bytes 663560 | tf_op jit(solution)/shard_map/ppermute | solution.py:155
  82.4 2.6 %copy-start.16 = (bf16[96,3,384]{2,1,0:T(4,128)(2,1)}, bf16[96,3,384]{2,1,0:T(4,128)(2,1)S(1)}, u32[]{:S(2)}) copy-start(bf16[96,3,384]{2,1,0:T(4,128)(2,1)S(1)} %collective-permute-done.4) | copy-start | bytes 663556
  84.9 0.8 copy-start.17
  85.7 16.9 %copy-start.4 = (f32[1,384]{1,0:T(1,128)S(1)}, f32[1,384]{1,0:T(1,128)}, u32[]{:S(2)}) copy-start(f32[1,384]{1,0:T(1,128)} %get-tuple-element.43.gain_ref) | copy-start | bytes 4612
  85.7 6.8 %collective-permute-start.6 = (bf16[3,38,384]{2,1,0:T(8,128)(2,1)}, bf16[3,38,384]{2,1,0:T(8,128)(2,1)}, u32[]{:S(2)}, u32[]{:S(2)}) collective-permute-start(bf16[3,38,384]{2,1,0:T(8,128)(2,1)} %get-tuple-element.7), channel_id=1, source_target_pairs={{0,32},{32,64},{64,96},{1,33},{33,65},{65,97},{2,34},{34,66},{66,9... | collective-permute-start | bytes 262664 | tf_op jit(solution)/shard_map/ppermute | solution.py:157
  89.1 7.7 %collective-permute-start.7 = (bf16[3,38,384]{2,1,0:T(8,128)(2,1)}, bf16[3,38,384]{2,1,0:T(8,128)(2,1)}, u32[]{:S(2)}, u32[]{:S(2)}) collective-permute-start(bf16[3,38,384]{2,1,0:T(8,128)(2,1)} %get-tuple-element.8), channel_id=1, source_target_pairs={{32,0},{64,32},{96,64},{33,1},{65,33},{97,65},{34,2},{66,34},{98,6... | collective-permute-start | bytes 262664 | tf_op jit(solution)/shard_map/ppermute | solution.py:158
  92.5 10.1 %copy-start.2 = (f32[49,384]{1,0:T(8,128)S(1)}, f32[49,384]{1,0:T(8,128)}, u32[]{:S(2)}) copy-start(f32[49,384]{1,0:T(8,128)} %reshape_squeeze.7.dw_ref) | copy-start | bytes 225796
  103.3 0.7 copy-start.6
  103.9 0.7 copy-start.11
  130.5 6.7 %collective-permute-start.8 = (bf16[1,32,384]{2,1,0:T(8,128)(2,1)S(1)}, bf16[1,32,384]{2,1,0:T(8,128)(2,1)S(1)}, u32[]{:S(2)}, u32[]{:S(2)}) collective-permute-start(bf16[1,32,384]{2,1,0:T(8,128)(2,1)S(1)} %slice.151), channel_id=1, source_target_pairs={{32,0},{64,32},{96,64},{33,1},{65,33},{97,65},{34,2},{66,34},{98,6... | collective-permute-start | bytes 73736 | tf_op jit(solution)/shard_map/ppermute | solution.py:164
  139.1 7.0 %copy-start.15 = (bf16[3,3,384,192]{2,3,1,0:T(8,128)(2,1)S(1)}, bf16[3,3,384,192]{2,3,1,0:T(8,128)(2,1)}, u32[]{:S(2)}) copy-start(bf16[3,3,384,192]{2,3,1,0:T(8,128)(2,1)} %param.24) | copy-start | bytes 3981316
  139.1 45.4 %all-to-all-start = ((bf16[32,4,32,384]{3,2,1,0:T(8,128)(2,1)}), bf16[32,4,32,384]{3,2,1,0:T(8,128)(2,1)}, u32[]{:S(2)}, u32[]{:S(2)}) async-start(bf16[32,4,32,384]{3,2,1,0:T(8,128)(2,1)} %maximum_maximum_fusion), calls=%async_computation | async-start | bytes 6291456 | tf_op jit(solution)/shard_map/all_to_all | solution.py:168
  147.7 39.0 %copy-start.13 = (f32[192]{0:T(256)S(1)}, f32[192]{0:T(256)}, u32[]{:S(2)}) copy-start(f32[192]{0:T(256)} %param.25) | copy-start | bytes 2308
  (2 other events, 1.3 us)

commit v2 on v1

v2 whole, which is shorter than its diff:
```python
import jax
import jax.numpy as jnp
from jax import lax
from jax.experimental import pallas as pl
from jax.experimental.pallas import tpu as pltpu
from jax.sharding import PartitionSpec as P

TS = 32
COL0 = 8
MESH = pl.DeviceIdType.MESH
F32 = jnp.float32
BF16 = jnp.bfloat16


def depthwise_block(x_ref, wb_ref, bias_ref, d_ref, row0, rows, groups):
    for g in range(groups):
        for cb in range(4):
            total = jnp.zeros((rows, 8, 128), F32)
            for b in range(7):
                start = COL0 - 3 + b + 8 * cb
                window = x_ref[g, pl.ds(row0, rows + 6), start : start + 8, :]
                for a in range(7):
                    total = total + window[a : a + rows] * wb_ref[a * 7 + b, g]
            d_ref[g, :, 8 * cb : 8 * cb + 8, :] = total + bias_ref[g]


def mix_block(depth, gain, shift, w_in, b_in, w_out, b_out):
    center = jnp.mean(depth, -1, keepdims=True)
    offset = depth - center
    spread = jnp.mean(offset * offset, -1, keepdims=True)
    normed = (offset * lax.rsqrt(spread + 1e-06) * gain + shift).astype(BF16)
    hidden = jnp.dot(normed, w_in, preferred_element_type=F32) + b_in
    inner = hidden * (0.7978845608028654 + 0.035677408136300125 * (hidden * hidden))
    half = 0.5 * hidden
    hidden = (half + half * jnp.tanh(inner)).astype(BF16)
    return jnp.dot(hidden, w_out, preferred_element_type=F32) + b_out


def swap_halves(v):
    return jnp.concatenate([v[..., 4:, :], v[..., :4, :]], -2)


def first_half(shape):
    return lax.broadcasted_iota(jnp.int32, shape, len(shape) - 2) < 4


def pack_edges(low, high):
    rows, _, channels = low.shape
    low = low.reshape(rows // 2, 2, 8, channels)
    high = high.reshape(rows // 2, 2, 8, channels)
    pick = first_half((rows // 2, 8, channels))
    left = jnp.where(pick, low[:, 0], swap_halves(low[:, 1]))
    right = jnp.where(pick, swap_halves(high[:, 0]), high[:, 1])
    return [v.reshape(rows * 4, channels).astype(BF16) for v in (left, right)]


def section_kernel(tiles_ref, coarse_ref, dw_ref, dwb_ref, gain_ref, shift_ref, win_ref, bin_ref, wout_ref,
                   bout_ref, scale_ref, y_ref, x_ref, wb_ref, d_ref, u_ref, out_ref, edge_out, edge_in,
                   row_out, row_in, corner_in, halo_send, halo_recv, sems, group_sems):
    height, width, channels = coarse_ref.shape
    groups = channels // 128
    lat, lon = lax.axis_index("lat"), lax.axis_index("lon")
    nlat, nlon = lax.axis_size("lat"), lax.axis_size("lon")
    left, right = lax.rem(lon + nlon - 1, nlon), lax.rem(lon + 1, nlon)
    has_up, has_down = lat > 0, lat < nlat - 1
    owned = height // nlon
    rows = d_ref.shape[2]
    blocks = TS // rows

    barrier = pltpu.get_barrier_semaphore()

    def greet(a, b):
        pl.semaphore_signal(barrier, inc=1, device_id=(a, b), device_id_type=MESH)

    @pl.loop(1, nlon)
    def _(k):
        greet(lat, lax.rem(lon + k, nlon))

    for present, other in ((has_up, lat - 1), (has_down, lat + 1)):
        @pl.when(present)
        def _():
            for b in (left, lon, right):
                greet(other, b)

    @pl.when(jnp.logical_and(has_down, lon == nlon - 1))
    def _():
        @pl.loop(0, nlon)
        def _(k):
            greet(lat + 1, k)

    def edge_copies(l, row0, count):
        part = pl.ds(pl.multiple_of(row0 * 4, 16), count * 4)
        return [pltpu.make_async_remote_copy(
            src_ref=edge_out.at[l, k, part], dst_ref=edge_in.at[l, k, part],
            send_sem=halo_send.at[l, k], recv_sem=halo_recv.at[l, k],
            device_id=(lat, (left, right)[k]), device_id_type=MESH) for k in range(2)]

    def row_copies(l, k):
        other = lat - 1 if k == 0 else lat + 1
        part = pl.ds(0, 16) if k == 0 else pl.ds(height * 4 - 16, 16)
        copies = [pltpu.make_async_remote_copy(
            src_ref=row_out.at[l, k], dst_ref=row_in.at[l, k],
            send_sem=halo_send.at[l, 2 + k], recv_sem=halo_recv.at[l, 2 + k],
            device_id=(other, lon), device_id_type=MESH)]
        for e in range(2):
            copies.append(pltpu.make_async_remote_copy(
                src_ref=edge_out.at[l, e, part], dst_ref=corner_in.at[l, k, e],
                send_sem=halo_send.at[l, 4 + 2 * k + e], recv_sem=halo_recv.at[l, 4 + 2 * k + e],
                device_id=(other, (left, right)[e]), device_id_type=MESH))
        return copies

    m0, m1, m2 = tiles_ref[0, 0], tiles_ref[1, 0], tiles_ref[2, 0]
    first_tile = jnp.where(m0 != 0, 0, 1)
    second_tile = jnp.where(m2 != 0, 2, 1)
    masks = [m.astype(F32) for m in (m0, m1, m2)]

    @pl.loop(0, height // 8)
    def _(i):
        part = pl.ds(pl.multiple_of(i * 8, 8), 8)
        low = coarse_ref[part, 0:16, :].astype(F32)[:, 0:8]
        high = coarse_ref[part, width - 16 : width, :].astype(F32)[:, 8:16]
        packed = pack_edges(low, high)
        for k in range(2):
            edge_out[0, k, pl.ds(pl.multiple_of(i * 32, 32), 32)] = packed[k]

    row_out[0, 0] = coarse_ref[0:3]
    row_out[0, 1] = coarse_ref[height - 3 : height]

    pl.semaphore_wait(barrier, nlon - 1 + jnp.where(has_up, 4, 0) + jnp.where(has_down, 3, 0))
    for copy in edge_copies(0, 0, height):
        copy.start()
    for k, present in enumerate((has_up, has_down)):
        @pl.when(present)
        def _():
            for copy in row_copies(0, k):
                copy.start()

    @pl.loop(0, height // 8)
    def _(i):
        part = pl.ds(pl.multiple_of(i * 8, 8), 8)
        for g in range(groups):
            x_ref[0, g, pl.ds(i * 8 + 3, 8), COL0 : COL0 + width, :] = coarse_ref[
                part, :, 128 * g : 128 * g + 128].astype(F32)

    def chunk_copy(row, slot, a, b, which):
        return pltpu.make_async_remote_copy(
            src_ref=out_ref.at[row], dst_ref=y_ref.at[slot, pl.ds(pl.multiple_of(lon * width, 32), width)],
            send_sem=group_sems.at[0, which], recv_sem=group_sems.at[1, which],
            device_id=(a, b), device_id_type=MESH)

    def own_copy(row, slot):
        return pltpu.make_async_copy(
            out_ref.at[row], y_ref.at[slot, pl.ds(pl.multiple_of(lon * width, 32), width)], sems.at[slot])

    def send_row(row):
        owner = row // owned
        slot = row - owner * owned

        @pl.when(owner == lon)
        def _():
            own_copy(row, slot).start()

        @pl.when(owner != lon)
        def _():
            chunk_copy(row, slot, lat, owner, 0).start()

        @pl.when(slot == 0)
        def _():
            @pl.when(row == 0)
            def _():
                @pl.when(has_up)
                def _():
                    chunk_copy(row, owned, lat - 1, nlon - 1, 1).start()

            @pl.when(row > 0)
            def _():
                @pl.when(owner - 1 == lon)
                def _():
                    own_copy(row, owned).start()

                @pl.when(owner - 1 != lon)
                def _():
                    chunk_copy(row, owned, lat, owner - 1, 1).start()

    for l in range(2):
        x = x_ref.at[l]
        for k in range(49):
            for g in range(groups):
                wb_ref[k, g] = jnp.broadcast_to(dw_ref[l, k : k + 1, 128 * g : 128 * g + 128], (8, 128))

        for copy in edge_copies(l, 0, height):
            copy.wait()

        @pl.loop(0, height // 8)
        def _(i):
            part = pl.ds(pl.multiple_of(i * 32, 32), 32)
            place = pl.ds(3 + i * 8, 8)
            after = edge_in[l, 0, part].astype(F32).reshape(4, 8, channels)
            before = edge_in[l, 1, part].astype(F32).reshape(4, 8, channels)
            after = jnp.stack([after, swap_halves(after)], 1).reshape(8, 8, channels)
            before = jnp.stack([swap_halves(before), before], 1).reshape(8, 8, channels)
            for g in range(groups):
                lanes = slice(128 * g, 128 * g + 128)
                x[g, place, COL0 + width : COL0 + width + 8, :] = after[:, :, lanes]
                x[g, place, 0:8, :] = before[:, :, lanes]

        for k, present in enumerate((has_up, has_down)):
            receives = (has_down, has_up)[k]
            place = height + 3 if k == 0 else 0

            @pl.when(present)
            def _():
                for copy in row_copies(l, k):
                    copy.wait_send()

            @pl.when(receives)
            def _():
                for copy in row_copies(l, k):
                    copy.wait_recv()
                middle = row_in[l, k].astype(F32)
                after = corner_in[l, k, 0].astype(F32).reshape(2, 8, channels)
                before = corner_in[l, k, 1].astype(F32).reshape(2, 8, channels)
                for g in range(groups):
                    lanes = slice(128 * g, 128 * g + 128)
                    x[g, place : place + 3, COL0 : COL0 + width, :] = middle[:, :, lanes]
                    for r in range(3):
                        n = r if k == 0 else r + 1
                        right_part = after[n // 2, :, lanes]
                        left_part = before[n // 2, :, lanes]
                        if n % 2:
                            right_part = swap_halves(right_part)
                        else:
                            left_part = swap_halves(left_part)
                        x[g, place + r, COL0 + width : COL0 + width + 8, :] = right_part
                        x[g, place + r, 0:8, :] = left_part

            @pl.when(jnp.logical_not(receives))
            def _():
                for g in range(groups):
                    x[g, place : place + 3] = jnp.zeros((3, width + 16, 128), F32)

        @pl.loop(0, blocks)
        def _(step):
            i = step if l == 0 else lax.rem(step + lon, blocks)

            @pl.loop(0, 2)
            def _(s):
                tile = jnp.where(s == 0, first_tile, second_tile)
                depthwise_block(x, wb_ref, dwb_ref.at[l], d_ref.at[s], tile * TS + i * rows, rows, groups)

            @pl.loop(0, 2)
            def _(s):
                depth = jnp.concatenate([d_ref[s, g].reshape(rows * width, 128) for g in range(groups)], 1)
                u_ref[s] = mix_block(depth, gain_ref[l], shift_ref[l], win_ref[l], bin_ref[l], wout_ref[l],
                                     bout_ref[l]).reshape(rows, width, channels)

            for t in range(3):
                row0 = pl.multiple_of(t * TS + i * rows, rows)
                place = pl.ds(3 + row0, rows)
                for g in range(groups):
                    lanes = slice(128 * g, 128 * g + 128)
                    if t == 1:
                        update = jnp.where(m0 == 0, u_ref[0, :, :, lanes], u_ref[1, :, :, lanes])
                    else:
                        update = u_ref[t // 2, :, :, lanes]
                    field = x[g, place, COL0 : COL0 + width, :]
                    field = (field + (masks[t] * scale_ref[l][:, lanes]) * update).astype(BF16)
                    out_ref[pl.ds(row0, rows), :, lanes] = field
                    if l == 0:
                        x_ref[1, g, place, COL0 : COL0 + width, :] = field.astype(F32)
            if l == 0:
                for t in range(3):
                    row0 = pl.multiple_of(t * TS + i * rows, rows)
                    low = out_ref[pl.ds(row0, rows), 0:16, :].astype(F32)[:, 0:8]
                    high = out_ref[pl.ds(row0, rows), width - 16 : width, :].astype(F32)[:, 8:16]
                    packed = pack_edges(low, high)
                    for k in range(2):
                        edge_out[1, k, pl.ds(pl.multiple_of(row0 * 4, 32), rows * 4)] = packed[k]
                    for copy in edge_copies(1, row0, rows):
                        copy.start()
            else:
                @pl.loop(0, 3 * rows)
                def _(n):
                    t = n // rows
                    send_row(t * TS + i * rows + n - t * rows)

        if l == 0:
            row_out[1, 0] = out_ref[0:3]
            row_out[1, 1] = out_ref[height - 3 : height]
            for k, present in enumerate((has_up, has_down)):
                @pl.when(present)
                def _():
                    for copy in row_copies(1, k):
                        copy.start()

    far = (nlon - 1) * width

    def count_wait(which, sem, n):
        copy = pltpu.make_async_copy(y_ref.at[owned, pl.ds(0, n * width)], y_ref.at[owned, pl.ds(0, n * width)],
                                     group_sems.at[which, sem])
        copy.wait()

    for which in range(2):
        pltpu.make_async_copy(y_ref.at[pl.ds(0, owned), pl.ds(0, far)], y_ref.at[pl.ds(0, owned), pl.ds(0, far)],
                              group_sems.at[which, 0]).wait()
    last = lon == nlon - 1
    sent = nlon - 2 + jnp.where(last, 1, 0) + jnp.where(has_up, 1, 0)
    for n in (nlon - 2, nlon - 1, nlon):
        @pl.when(sent == n)
        def _():
            count_wait(0, 1, n)

    @pl.when(jnp.logical_not(last))
    def _():
        count_wait(1, 1, nlon - 1)

    @pl.when(jnp.logical_and(last, has_down))
    def _():
        count_wait(1, 1, nlon)

    for slot in range(owned):
        own_copy(slot, slot).wait()

    @pl.when(jnp.logical_not(last))
    def _():
        own_copy(0, owned).wait()


def section_call(tiles, coarse, dw, dwb, gain, shift, win, b_in, wout, bout, scale, rows=8):
    height, width, channels = coarse.shape
    groups = channels // 128
    nlon = lax.axis_size("lon")
    owned = height // nlon
    vmem = pl.BlockSpec(memory_space=pltpu.VMEM)
    dma = pltpu.SemaphoreType.DMA
    return pl.pallas_call(
        section_kernel,
        out_shape=jax.ShapeDtypeStruct((owned + 1, nlon * width, channels), BF16),
        in_specs=[pl.BlockSpec(memory_space=pltpu.SMEM)] + [vmem] * 10,
        out_specs=pl.BlockSpec(memory_space=pl.ANY),
        scratch_shapes=[
            pltpu.VMEM((2, groups, height + 6, width + 16, 128), F32),
            pltpu.VMEM((49, groups, 8, 128), F32),
            pltpu.VMEM((2, groups, rows, width, 128), F32),
            pltpu.VMEM((2, rows, width, channels), F32),
            pltpu.VMEM((height, width, channels), BF16),
            pltpu.VMEM((2, 2, height * 4, channels), BF16),
            pltpu.VMEM((2, 2, height * 4, channels), BF16),
            pltpu.VMEM((2, 2, 3, width, channels), BF16),
            pltpu.VMEM((2, 2, 3, width, channels), BF16),
            pltpu.VMEM((2, 2, 2, 16, channels), BF16),
            dma((2, 8)),
            dma((2, 8)),
            dma((owned + 1,)),
            dma((2, 2)),
        ],
        compiler_params=pltpu.CompilerParams(
            collective_id=0, has_side_effects=True, vmem_limit_bytes=50 * 1024 * 1024),
        cost_estimate=pl.CostEstimate(flops=12_000_000_000, bytes_accessed=10_000_000, transcendentals=0),
    )(tiles, coarse, dw, dwb, gain, shift, win, b_in, wout, bout, scale)


UCH = 512


def nt(w, y):
    return lax.dot_general(w, y, (((1,), (1,)), ((), ())), preferred_element_type=F32)


def upsample_kernel(valid_ref, y_ref, next_ref, wt_ref, bias_ref, out_ref):
    width_out = out_ref.shape[1]
    row = lax.broadcasted_iota(jnp.int32, (256, 256), 0)
    col = lax.broadcasted_iota(jnp.int32, (256, 256), 1)
    order = jnp.where(row == (col % 2) * 128 + col // 2, 1.0, 0.0).astype(BF16)
    direct, beside = [], []
    for i in range(4):
        cur, after = y_ref[i], next_ref[i]
        if i == 3:
            valid = valid_ref[0] != 0
            cur = jnp.where(valid, cur, jnp.zeros_like(cur))
            after = jnp.where(valid, after, jnp.zeros_like(after))
        both = jnp.concatenate([cur, after], 0).astype(F32)
        right = both[1 : 1 + UCH].astype(BF16)
        begin, end = (4 if i == 3 else 0, 4 if i == 0 else 6)
        values = nt(wt_ref[begin * width_out : end * width_out], cur)
        direct.append({begin + n: values[n * width_out : (n + 1) * width_out] for n in range(end - begin)})
        begin, end = (8 if i == 3 else 6, 8 if i == 0 else 9)
        values = nt(wt_ref[begin * width_out : end * width_out], right)
        beside.append({begin + n: values[n * width_out : (n + 1) * width_out] for n in range(end - begin)})
    bias = bias_ref[...]
    for i in range(3):
        ee = direct[i][0] + bias
        eo = direct[i][1] + beside[i][6] + bias
        oe = direct[i][2] + direct[i + 1][4] + bias
        oo = direct[i][3] + beside[i][7] + direct[i + 1][5] + beside[i + 1][8] + bias
        for p, (even, odd) in enumerate(((ee, eo), (oe, oo))):
            even, odd = even.astype(BF16), odd.astype(BF16)
            for k in range(UCH // 128):
                lanes = slice(128 * k, 128 * k + 128)
                pair = jnp.concatenate([even[:, lanes], odd[:, lanes]], 1)
                out_ref[2 * i + p, :, 256 * k : 256 * k + 256] = jnp.dot(
                    pair, order, preferred_element_type=F32).astype(BF16)


def upsample_call(valid, y, weight, bias):
    rows, width, channels = y.shape
    out_width = weight.shape[3]
    wt = weight.transpose(0, 1, 3, 2).reshape(9, out_width, channels)
    wt = jnp.concatenate([wt[4:6], wt[7:9], wt[1:3], wt[3:4], wt[6:7], wt[0:1]]).reshape(-1, channels)
    chunks = width // UCH
    bias = jnp.broadcast_to(bias.reshape(-1, 1), (out_width, UCH))
    whole = lambda w: pl.BlockSpec(w.shape, lambda j: (0,) * w.ndim)
    out = pl.pallas_call(
        upsample_kernel,
        grid=(chunks,),
        out_shape=jax.ShapeDtypeStruct((2 * rows - 2, out_width, 2 * width), BF16),
        in_specs=[
            pl.BlockSpec(memory_space=pltpu.SMEM),
            pl.BlockSpec((rows, UCH, channels), lambda j: (0, j, 0)),
            pl.BlockSpec((rows, 16, channels), lambda j: (0, ((j + 1) % chunks) * (UCH // 16), 0)),
            whole(wt), whole(bias),
        ],
        out_specs=pl.BlockSpec((2 * rows - 2, out_width, 2 * UCH), lambda j: (0, 0, j)),
        compiler_params=pltpu.CompilerParams(vmem_limit_bytes=48 * 1024 * 1024),
    )(valid, y, y, wt, bias)
    return out.transpose(0, 2, 1)


def local(coarse, ocean_tiles, dw_weight, dw_bias, norm_gain, norm_shift, in_weight, in_bias,
          out_weight, out_bias, layer_scale, up_weight, up_bias):
    channels = coarse.shape[2]
    row = lambda v: v[:, None, :]
    rows = section_call(ocean_tiles, coarse, dw_weight.reshape(2, 49, channels),
                        dw_bias.reshape(2, channels // 128, 1, 128), row(norm_gain), row(norm_shift), in_weight,
                        row(in_bias), out_weight, row(out_bias), row(layer_scale))
    end = jnp.logical_and(lax.axis_index("lat") == lax.axis_size("lat") - 1,
                          lax.axis_index("lon") == lax.axis_size("lon") - 1)
    valid = jnp.where(end, 0, 1).astype(jnp.int32).reshape(1)
    return upsample_call(valid, rows, up_weight, up_bias)


def solution(mesh):
    placed = (P("lat", "lon", None), P("lat", "lon")) + (P(),) * 11
    return jax.shard_map(
        local, mesh=mesh, in_specs=placed, out_specs=P(("lat", "lon"), None, None), check_vma=False
    )
```

time: 205 us -> 134 us (0.65)
  the two profiles are of different devices: /device:TPU:1 before, /device:TPU:29 now
where the time goes in v2:
time: 134 us; the launch traced here: 133 us
  Pallas kernels  120 us (90%)
  local copies, waits for them, and re-layouts  13.6 us (10%)
    pallas_call x1, Pallas kernels, section_call(): pl.pallas_call(section_kernel, out_shape=jax.ShapeDtypeStruct((owned + 1,...  111 us
    pallas_call x1, Pallas kernels, upsample_call(): pl.pallas_call(upsample_kernel, grid=(chunks,), out_shape=jax.ShapeDtypeS...  9.01 us
    unnamed x11, local copies, waits for them, and re-layouts  6.82 us
    broadcast_in_dim x5, local copies, waits for them, and re-layouts, local(): row = lambda v: v[:, None, :]  3.44 us

profile of v2, /device:TPU:29, one launch (start us, length us, event | category | flops | bytes accessed | tf_op | source)
XLA Modules:
  0.0 133.2 jit_solution(9605914509507569482)
XLA Ops:
  0.0 0.7 copy.16.tiles_ref
  0.7 0.7 reshape.19.dwb_ref
  1.4 0.7 broadcast_in_dim.20.gain_ref
  2.1 0.7 broadcast_in_dim.21.shift_ref
  2.8 0.7 broadcast_in_dim.23.bout_ref
  3.5 0.7 broadcast_in_dim.24.scale_ref
  4.2 0.7 broadcast_in_dim.22.bin_ref
  4.9 0.9 copy.17.dw_ref
  5.8 0.8 broadcast_in_dim.25.bias_ref
  6.6 0.0 copy-start.1
  6.6 0.0 copy-start.2
  6.6 1.1 slice_dynamic-update-slice_fusion.2
  7.8 1.0 slice_dynamic-update-slice_fusion.1
  8.8 1.1 slice_dynamic-update-slice_fusion
  9.9 0.9 slice_dynamic-update-slice_fusion.4
  10.8 0.9 slice_dynamic-update-slice_fusion.3
  11.7 0.0 copy-done.1
  11.8 0.0 copy-done.2
  11.8 110.5 %shard_map.127.y_ref.next_ref = bf16[4,1024,384]{2,1,0:T(8,128)(2,1)} custom-call(s32[3,1]{1,0:T(4,128)S(1)} %copy.16.tiles_ref, bf16[96,32,384]{2,1,0:T(8,128)(2,1)} %coarse_ref.1, f32[2,49,384]{2,1,0:T(8,128)S(1)} %copy.17.dw_ref, f32[2,3,1,128]{3,2,1,0:T(1,128)S(1)} %reshape.19.dwb_ref, f32[2,1,384]{2,1,0:T(1,128)S(1)} %broadcast_in_dim.20.gain_ref, ...), custom_call_target="tpu_custom_call" | custom-call | flops 12000000000 | bytes 10000000 | tf_op jit(solution)/shard_map/pallas_call | solution.py:336
  122.3 0.0 copy-start
  122.3 1.9 %copy-done = bf16[4,1024,384]{2,1,0:T(8,128)(2,1)S(1)} copy-done((bf16[4,1024,384]{2,1,0:T(8,128)(2,1)S(1)}, bf16[4,1024,384]{2,1,0:T(8,128)(2,1)}, u32[]{:S(2)}) %copy-start) | copy-done | bytes 3145752
  124.2 9.0 %shard_map.128 = bf16[6,192,2048]{2,1,0:T(8,128)(2,1)} custom-call(s32[1]{0:T(128)} %bitcast.valid_ref, bf16[4,1024,384]{2,1,0:T(8,128)(2,1)S(1)} %copy-done, bf16[4,1024,384]{2,1,0:T(8,128)(2,1)S(1)} %copy-done, bf16[1728,384]{1,0:T(8,128)(2,1)S(1)} %bitcast.7, f32[192,512]{1,0:T(8,128)S(1)} %broadcast_in_dim.25.bias_ref), custom_call_target="tpu_custom_call" | custom-call | tf_op jit(solution)/shard_map/pallas_call | solution.py:413
Async XLA Ops:
  6.6 5.2 %copy-start.1 = (bf16[2,384,768]{2,1,0:T(8,128)(2,1)S(1)}, bf16[2,384,768]{2,1,0:T(8,128)(2,1)}, u32[]{:S(2)}) copy-start(bf16[2,384,768]{2,1,0:T(8,128)(2,1)} %win_ref.1) | copy-start | bytes 3538948
  6.6 5.2 %copy-start.2 = (bf16[2,768,384]{2,1,0:T(8,128)(2,1)S(1)}, bf16[2,768,384]{2,1,0:T(8,128)(2,1)}, u32[]{:S(2)}) copy-start(bf16[2,768,384]{2,1,0:T(8,128)(2,1)} %wout_ref.1) | copy-start | bytes 3538948
  122.3 1.9 %copy-start = (bf16[4,1024,384]{2,1,0:T(8,128)(2,1)S(1)}, bf16[4,1024,384]{2,1,0:T(8,128)(2,1)}, u32[]{:S(2)}) copy-start(bf16[4,1024,384]{2,1,0:T(8,128)(2,1)} %shard_map.127.y_ref.next_ref) | copy-start | bytes 9437188

commit v3 on v2

--- a/solution.py
+++ b/solution.py
@@ -12,16 +12,16 @@
 BF16 = jnp.bfloat16
 
 
-def depthwise_block(x_ref, wb_ref, bias_ref, d_ref, row0, rows, groups):
+def depthwise_block(x_ref, wb_ref, bias_ref, l, d_ref, row0, rows, groups, parts):
     for g in range(groups):
-        for cb in range(4):
+        for cb in parts:
             total = jnp.zeros((rows, 8, 128), F32)
             for b in range(7):
                 start = COL0 - 3 + b + 8 * cb
                 window = x_ref[g, pl.ds(row0, rows + 6), start : start + 8, :]
                 for a in range(7):
                     total = total + window[a : a + rows] * wb_ref[a * 7 + b, g]
-            d_ref[g, :, 8 * cb : 8 * cb + 8, :] = total + bias_ref[g]
+            d_ref[g, :, 8 * cb : 8 * cb + 8, :] = total + bias_ref[l : l + 1, 128 * g : 128 * g + 128]
 
 
 def mix_block(depth, gain, shift, w_in, b_in, w_out, b_out):
@@ -64,7 +64,7 @@
     left, right = lax.rem(lon + nlon - 1, nlon), lax.rem(lon + 1, nlon)
     has_up, has_down = lat > 0, lat < nlat - 1
     owned = height // nlon
-    rows = d_ref.shape[2]
+    rows = u_ref.shape[1]
     blocks = TS // rows
 
     barrier = pltpu.get_barrier_semaphore()
@@ -109,7 +109,7 @@
                 device_id=(other, (left, right)[e]), device_id_type=MESH))
         return copies
 
-    m0, m1, m2 = tiles_ref[0, 0], tiles_ref[1, 0], tiles_ref[2, 0]
+    m0, m1, m2 = tiles_ref[0, 0], tiles_ref[0, 1], tiles_ref[0, 2]
     first_tile = jnp.where(m0 != 0, 0, 1)
     second_tile = jnp.where(m2 != 0, 2, 1)
     masks = [m.astype(F32) for m in (m0, m1, m2)]
@@ -127,13 +127,13 @@
     row_out[0, 1] = coarse_ref[height - 3 : height]
 
     pl.semaphore_wait(barrier, nlon - 1 + jnp.where(has_up, 4, 0) + jnp.where(has_down, 3, 0))
+    for k, present in enumerate((has_up, has_down)):
+        @pl.when(present)
+        def _():
+            for copy in row_copies(0, k):
+                copy.start()
     for copy in edge_copies(0, 0, height):
         copy.start()
-    for k, present in enumerate((has_up, has_down)):
-        @pl.when(present)
-        def _():
-            for copy in row_copies(0, k):
-                copy.start()
 
     @pl.loop(0, height // 8)
     def _(i):
@@ -184,25 +184,30 @@
 
     for l in range(2):
         x = x_ref.at[l]
+        one = slice(l, l + 1)
         for k in range(49):
             for g in range(groups):
-                wb_ref[k, g] = jnp.broadcast_to(dw_ref[l, k : k + 1, 128 * g : 128 * g + 128], (8, 128))
-
-        for copy in edge_copies(l, 0, height):
-            copy.wait()
-
-        @pl.loop(0, height // 8)
-        def _(i):
-            part = pl.ds(pl.multiple_of(i * 32, 32), 32)
-            place = pl.ds(3 + i * 8, 8)
-            after = edge_in[l, 0, part].astype(F32).reshape(4, 8, channels)
-            before = edge_in[l, 1, part].astype(F32).reshape(4, 8, channels)
-            after = jnp.stack([after, swap_halves(after)], 1).reshape(8, 8, channels)
-            before = jnp.stack([swap_halves(before), before], 1).reshape(8, 8, channels)
-            for g in range(groups):
-                lanes = slice(128 * g, 128 * g + 128)
-                x[g, place, COL0 + width : COL0 + width + 8, :] = after[:, :, lanes]
-                x[g, place, 0:8, :] = before[:, :, lanes]
+                wb_ref[k, g] = jnp.broadcast_to(dw_ref[k // 7, k % 7, l : l + 1, 128 * g : 128 * g + 128], (8, 128))
+
+        def place_edges():
+            for copy in edge_copies(l, 0, height):
+                copy.wait()
+
+            @pl.loop(0, height // 8)
+            def _(i):
+                part = pl.ds(pl.multiple_of(i * 32, 32), 32)
+                place = pl.ds(3 + i * 8, 8)
+                after = edge_in[l, 0, part].astype(F32).reshape(4, 8, channels)
+                before = edge_in[l, 1, part].astype(F32).reshape(4, 8, channels)
+                after = jnp.stack([after, swap_halves(after)], 1).reshape(8, 8, channels)
+                before = jnp.stack([swap_halves(before), before], 1).reshape(8, 8, channels)
+                for g in range(groups):
+                    lanes = slice(128 * g, 128 * g + 128)
+                    x[g, place, COL0 + width : COL0 + width + 8, :] = after[:, :, lanes]
+                    x[g, place, 0:8, :] = before[:, :, lanes]
+
+        if l == 1:
+            place_edges()
 
         for k, present in enumerate((has_up, has_down)):
             receives = (has_down, has_up)[k]
@@ -239,20 +244,31 @@
                 for g in range(groups):
                     x[g, place : place + 3] = jnp.zeros((3, width + 16, 128), F32)
 
-        @pl.loop(0, blocks)
-        def _(step):
-            i = step if l == 0 else lax.rem(step + lon, blocks)
-
+        def depthwise(i, parts):
             @pl.loop(0, 2)
             def _(s):
                 tile = jnp.where(s == 0, first_tile, second_tile)
-                depthwise_block(x, wb_ref, dwb_ref.at[l], d_ref.at[s], tile * TS + i * rows, rows, groups)
+                depthwise_block(x, wb_ref, dwb_ref, l, d_ref.at[s, :, pl.ds(pl.multiple_of(i * rows, rows), rows)],
+                                tile * TS + i * rows, rows, groups, parts)
+
+        if l == 0:
+            @pl.loop(0, blocks)
+            def _(i):
+                depthwise(i, (1, 2))
+
+            place_edges()
+
+        @pl.loop(0, blocks)
+        def _(step):
+            i = step if l == 0 else lax.rem(step + lon // 8, blocks)
+
+            depthwise(i, (0, 3) if l == 0 else (0, 1, 2, 3))
 
             @pl.loop(0, 2)
             def _(s):
-                depth = jnp.concatenate([d_ref[s, g].reshape(rows * width, 128) for g in range(groups)], 1)
-                u_ref[s] = mix_block(depth, gain_ref[l], shift_ref[l], win_ref[l], bin_ref[l], wout_ref[l],
-                                     bout_ref[l]).reshape(rows, width, channels)
+                depth = jnp.concatenate([d_ref[s, g, pl.ds(pl.multiple_of(i * rows, rows), rows)].reshape(rows * width, 128) for g in range(groups)], 1)
+                u_ref[s] = mix_block(depth, gain_ref[one], shift_ref[one], win_ref[l], bin_ref[one], wout_ref[l],
+                                     bout_ref[one]).reshape(rows, width, channels)
 
             for t in range(3):
                 row0 = pl.multiple_of(t * TS + i * rows, rows)
@@ -264,7 +280,7 @@
                     else:
                         update = u_ref[t // 2, :, :, lanes]
                     field = x[g, place, COL0 : COL0 + width, :]
-                    field = (field + (masks[t] * scale_ref[l][:, lanes]) * update).astype(BF16)
+                    field = (field + (masks[t] * scale_ref[one, lanes]) * update).astype(BF16)
                     out_ref[pl.ds(row0, rows), :, lanes] = field
                     if l == 0:
                         x_ref[1, g, place, COL0 : COL0 + width, :] = field.astype(F32)
@@ -281,8 +297,9 @@
             else:
                 @pl.loop(0, 3 * rows)
                 def _(n):
-                    t = n // rows
-                    send_row(t * TS + i * rows + n - t * rows)
+                    t = lax.rem(n, 3)
+                    r = lax.rem(n // 3 * 5 + lon // 4, rows)
+                    send_row(t * TS + i * rows + r)
 
         if l == 0:
             row_out[1, 0] = out_ref[0:3]
@@ -341,7 +358,7 @@
         scratch_shapes=[
             pltpu.VMEM((2, groups, height + 6, width + 16, 128), F32),
             pltpu.VMEM((49, groups, 8, 128), F32),
-            pltpu.VMEM((2, groups, rows, width, 128), F32),
+            pltpu.VMEM((2, groups, TS, width, 128), F32),
             pltpu.VMEM((2, rows, width, channels), F32),
             pltpu.VMEM((height, width, channels), BF16),
             pltpu.VMEM((2, 2, height * 4, channels), BF16),
@@ -355,7 +372,7 @@
             dma((2, 2)),
         ],
         compiler_params=pltpu.CompilerParams(
-            collective_id=0, has_side_effects=True, vmem_limit_bytes=50 * 1024 * 1024),
+            collective_id=0, has_side_effects=True, vmem_limit_bytes=60 * 1024 * 1024),
         cost_estimate=pl.CostEstimate(flops=12_000_000_000, bytes_accessed=10_000_000, transcendentals=0),
     )(tiles, coarse, dw, dwb, gain, shift, win, b_in, wout, bout, scale)
 
@@ -367,7 +384,17 @@
     return lax.dot_general(w, y, (((1,), (1,)), ((), ())), preferred_element_type=F32)
 
 
-def upsample_kernel(valid_ref, y_ref, next_ref, wt_ref, bias_ref, out_ref):
+TAPS = (4, 5, 7, 8, 1, 2, 3, 6, 0)
+
+
+def upsample_kernel(y_ref, next_ref, wt_ref, bias_ref, out_ref):
+    last = jnp.logical_and(lax.axis_index("lat") == lax.axis_size("lat") - 1,
+                           lax.axis_index("lon") == lax.axis_size("lon") - 1)
+    valid = jnp.logical_not(last)
+
+    def weights(begin, end):
+        return jnp.concatenate([wt_ref[n] for n in TAPS[begin:end]], 0)
+
     width_out = out_ref.shape[1]
     row = lax.broadcasted_iota(jnp.int32, (256, 256), 0)
     col = lax.broadcasted_iota(jnp.int32, (256, 256), 1)
@@ -376,18 +403,19 @@
     for i in range(4):
         cur, after = y_ref[i], next_ref[i]
         if i == 3:
-            valid = valid_ref[0] != 0
             cur = jnp.where(valid, cur, jnp.zeros_like(cur))
             after = jnp.where(valid, after, jnp.zeros_like(after))
         both = jnp.concatenate([cur, after], 0).astype(F32)
         right = both[1 : 1 + UCH].astype(BF16)
         begin, end = (4 if i == 3 else 0, 4 if i == 0 else 6)
-        values = nt(wt_ref[begin * width_out : end * width_out], cur)
+        values = nt(weights(begin, end), cur)
         direct.append({begin + n: values[n * width_out : (n + 1) * width_out] for n in range(end - begin)})
         begin, end = (8 if i == 3 else 6, 8 if i == 0 else 9)
-        values = nt(wt_ref[begin * width_out : end * width_out], right)
+        values = nt(weights(begin, end), right)
         beside.append({begin + n: values[n * width_out : (n + 1) * width_out] for n in range(end - begin)})
-    bias = bias_ref[...]
+    same = lax.broadcasted_iota(jnp.int32, (width_out, width_out), 0) == lax.broadcasted_iota(
+        jnp.int32, (width_out, width_out), 1)
+    bias = jnp.sum(jnp.where(same, bias_ref[...], 0.0), axis=1, keepdims=True)
     for i in range(3):
         ee = direct[i][0] + bias
         eo = direct[i][1] + beside[i][6] + bias
@@ -402,41 +430,33 @@
                     pair, order, preferred_element_type=F32).astype(BF16)
 
 
-def upsample_call(valid, y, weight, bias):
+def upsample_call(y, weight, bias):
     rows, width, channels = y.shape
     out_width = weight.shape[3]
     wt = weight.transpose(0, 1, 3, 2).reshape(9, out_width, channels)
-    wt = jnp.concatenate([wt[4:6], wt[7:9], wt[1:3], wt[3:4], wt[6:7], wt[0:1]]).reshape(-1, channels)
     chunks = width // UCH
-    bias = jnp.broadcast_to(bias.reshape(-1, 1), (out_width, UCH))
+    bias = bias.reshape(1, -1)
     whole = lambda w: pl.BlockSpec(w.shape, lambda j: (0,) * w.ndim)
     out = pl.pallas_call(
         upsample_kernel,
         grid=(chunks,),
         out_shape=jax.ShapeDtypeStruct((2 * rows - 2, out_width, 2 * width), BF16),
         in_specs=[
-            pl.BlockSpec(memory_space=pltpu.SMEM),
             pl.BlockSpec((rows, UCH, channels), lambda j: (0, j, 0)),
             pl.BlockSpec((rows, 16, channels), lambda j: (0, ((j + 1) % chunks) * (UCH // 16), 0)),
             whole(wt), whole(bias),
         ],
         out_specs=pl.BlockSpec((2 * rows - 2, out_width, 2 * UCH), lambda j: (0, 0, j)),
-        compiler_params=pltpu.CompilerParams(vmem_limit_bytes=48 * 1024 * 1024),
-    )(valid, y, y, wt, bias)
+        compiler_params=pltpu.CompilerParams(vmem_limit_bytes=60 * 1024 * 1024),
+    )(y, y, wt, bias)
     return out.transpose(0, 2, 1)
 
 
 def local(coarse, ocean_tiles, dw_weight, dw_bias, norm_gain, norm_shift, in_weight, in_bias,
           out_weight, out_bias, layer_scale, up_weight, up_bias):
-    channels = coarse.shape[2]
-    row = lambda v: v[:, None, :]
-    rows = section_call(ocean_tiles, coarse, dw_weight.reshape(2, 49, channels),
-                        dw_bias.reshape(2, channels // 128, 1, 128), row(norm_gain), row(norm_shift), in_weight,
-                        row(in_bias), out_weight, row(out_bias), row(layer_scale))
-    end = jnp.logical_and(lax.axis_index("lat") == lax.axis_size("lat") - 1,
-                          lax.axis_index("lon") == lax.axis_size("lon") - 1)
-    valid = jnp.where(end, 0, 1).astype(jnp.int32).reshape(1)
-    return upsample_call(valid, rows, up_weight, up_bias)
+    rows = section_call(ocean_tiles.T, coarse, dw_weight.transpose(1, 2, 0, 3), dw_bias, norm_gain, norm_shift,
+                        in_weight, in_bias, out_weight, out_bias, layer_scale)
+    return upsample_call(rows, up_weight, up_bias)
 
 
 def solution(mesh):

time: 134 us -> 104 us (0.78)
  the two profiles are of different devices: /device:TPU:29 before, /device:TPU:31 now
where the time goes in v3:
time: 104 us; the launch traced here: 103 us
  Pallas kernels  103 us (99%)
    pallas_call x1, Pallas kernels, section_call(): pl.pallas_call(section_kernel, out_shape=jax.ShapeDtypeStruct((owned + 1,...  93.1 us
    pallas_call x1, Pallas kernels, upsample_call(): pl.pallas_call(upsample_kernel, grid=(chunks,), out_shape=jax.ShapeDtypeS...  10.4 us

profile of v3, /device:TPU:31, one launch (start us, length us, event | category | flops | bytes accessed | tf_op | source)
XLA Modules:
  0.0 103.5 jit_solution(11141120004103018087)
XLA Ops:
  0.0 93.1 %shard_map.127.y_ref.next_ref = bf16[4,1024,384]{2,1,0:T(8,128)(2,1)} custom-call(s32[1,3]{1,0:T(1,128)} %bitcast.10, bf16[96,32,384]{2,1,0:T(8,128)(2,1)} %coarse_ref.1, f32[7,7,2,384]{3,2,1,0:T(2,128)} %bitcast.9, f32[2,384]{1,0:T(2,128)} %dwb_ref.1, f32[2,384]{1,0:T(2,128)} %gain_ref.1, f32[2,384]{1,0:T(2,128)} %shift_ref.1, ...), custom_call_target="tpu_custom_call" | custom-call | flops 12000000000 | bytes 10000000 | tf_op jit(solution)/shard_map/pallas_call | solution.py:353
  93.1 10.4 %shard_map.128 = bf16[6,192,2048]{2,1,0:T(8,128)(2,1)} custom-call(bf16[4,1024,384]{2,1,0:T(8,128)(2,1)} %shard_map.127.y_ref.next_ref, bf16[4,1024,384]{2,1,0:T(8,128)(2,1)} %shard_map.127.y_ref.next_ref, bf16[9,192,384]{2,1,0:T(8,128)(2,1)} %bitcast.7, f32[1,192]{1,0:T(1,128)} %bitcast.8), custom_call_target="tpu_custom_call" | custom-call | tf_op jit(solution)/shard_map/pallas_call | solution.py:440

commit v4 on v3

--- a/solution.py
+++ b/solution.py
@@ -1,3 +1,4 @@
+import functools
 import jax
 import jax.numpy as jnp
 from jax import lax
@@ -36,26 +37,39 @@
     return jnp.dot(hidden, w_out, preferred_element_type=F32) + b_out
 
 
-def swap_halves(v):
-    return jnp.concatenate([v[..., 4:, :], v[..., :4, :]], -2)
-
-
-def first_half(shape):
-    return lax.broadcasted_iota(jnp.int32, shape, len(shape) - 2) < 4
-
-
-def pack_edges(low, high):
-    rows, _, channels = low.shape
-    low = low.reshape(rows // 2, 2, 8, channels)
-    high = high.reshape(rows // 2, 2, 8, channels)
-    pick = first_half((rows // 2, 8, channels))
-    left = jnp.where(pick, low[:, 0], swap_halves(low[:, 1]))
-    right = jnp.where(pick, swap_halves(high[:, 0]), high[:, 1])
-    return [v.reshape(rows * 4, channels).astype(BF16) for v in (left, right)]
-
-
-def section_kernel(tiles_ref, coarse_ref, dw_ref, dwb_ref, gain_ref, shift_ref, win_ref, bin_ref, wout_ref,
-                   bout_ref, scale_ref, y_ref, x_ref, wb_ref, d_ref, u_ref, out_ref, edge_out, edge_in,
+CHUNK = 80
+
+
+def turned(v, shift):
+    return pltpu.roll(v, shift % 8, axis=0) if shift % 8 else v
+
+
+def pack_rows(lines, base):
+    place = lax.broadcasted_iota(jnp.int32, lines[0].shape, 0)
+    blocks = []
+    for k in range(3):
+        block = jnp.zeros_like(lines[0])
+        for r in range(8):
+            low = 3 * r - 8 * k
+            if low > -3 and low < 8:
+                inside = jnp.logical_and(place >= low, place < low + 3)
+                block = jnp.where(inside, turned(lines[r], low - base), block)
+        blocks.append(block)
+    return blocks
+
+
+def unpack_row(blocks, r, base):
+    first, last = 3 * r // 8, (3 * r + 2) // 8
+    value = turned(blocks[first], base - 3 * r + 8 * first)
+    if last != first:
+        place = lax.broadcasted_iota(jnp.int32, value.shape, 0)
+        other = turned(blocks[last], base - 3 * r + 8 * last)
+        value = jnp.where(place >= base + 8 * last - 3 * r, other, value)
+    return value
+
+
+def section_kernel(step_rows, tiles_ref, coarse_hbm, dw_hbm, dwb_ref, gain_ref, shift_ref, win_hbm, bin_ref, wout_hbm,
+                   bout_ref, scale_ref, y_ref, coarse_ref, dw_ref, win_ref, wout_ref, load_sems, x_ref, wb_ref, d_ref, u_ref, out_ref, edge_out, edge_in,
                    row_out, row_in, corner_in, halo_send, halo_recv, sems, group_sems):
     height, width, channels = coarse_ref.shape
     groups = channels // 128
@@ -64,8 +78,11 @@
     left, right = lax.rem(lon + nlon - 1, nlon), lax.rem(lon + 1, nlon)
     has_up, has_down = lat > 0, lat < nlat - 1
     owned = height // nlon
-    rows = u_ref.shape[1]
-    blocks = TS // rows
+
+    loads = [pltpu.make_async_copy(a, b, load_sems.at[n]) for n, (a, b) in enumerate((
+        (coarse_hbm, coarse_ref), (dw_hbm, dw_ref), (win_hbm, win_ref), (wout_hbm, wout_ref)))]
+    for load in loads:
+        load.start()
 
     barrier = pltpu.get_barrier_semaphore()
 
@@ -88,16 +105,28 @@
         def _(k):
             greet(lat + 1, k)
 
-    def edge_copies(l, row0, count):
-        part = pl.ds(pl.multiple_of(row0 * 4, 16), count * 4)
+    def edge_copies(l, chunk, count):
+        part = pl.ds(pl.multiple_of(chunk * CHUNK, CHUNK), count * CHUNK)
         return [pltpu.make_async_remote_copy(
             src_ref=edge_out.at[l, k, part], dst_ref=edge_in.at[l, k, part],
             send_sem=halo_send.at[l, k], recv_sem=halo_recv.at[l, k],
             device_id=(lat, (left, right)[k]), device_id_type=MESH) for k in range(2)]
 
+    def pack_edges(source, l, i):
+        low, high = [], []
+        for t in range(3):
+            part = pl.ds(pl.multiple_of(t * TS + i * 8, 8), 8)
+            begin = source[part, 0:16, :].astype(F32)
+            end = source[part, width - 16 : width, :].astype(F32)
+            low += pack_rows([begin[r, 0:8] for r in range(8)], 0)
+            high += pack_rows([end[r, 8:16] for r in range(8)], 5)
+        for k, blocks in enumerate((low, high)):
+            blocks = blocks + [jnp.zeros_like(blocks[0])]
+            edge_out[l, k, pl.ds(pl.multiple_of(i * CHUNK, CHUNK), CHUNK)] = jnp.concatenate(blocks, 0).astype(BF16)
+
     def row_copies(l, k):
         other = lat - 1 if k == 0 else lat + 1
-        part = pl.ds(0, 16) if k == 0 else pl.ds(height * 4 - 16, 16)
+        part = pl.ds(0, 32) if k == 0 else pl.ds(4 * CHUNK - 32, 32)
         copies = [pltpu.make_async_remote_copy(
             src_ref=row_out.at[l, k], dst_ref=row_in.at[l, k],
             send_sem=halo_send.at[l, 2 + k], recv_sem=halo_recv.at[l, 2 + k],
@@ -114,14 +143,11 @@
     second_tile = jnp.where(m2 != 0, 2, 1)
     masks = [m.astype(F32) for m in (m0, m1, m2)]
 
-    @pl.loop(0, height // 8)
+    loads[0].wait()
+
+    @pl.loop(0, 4)
     def _(i):
-        part = pl.ds(pl.multiple_of(i * 8, 8), 8)
-        low = coarse_ref[part, 0:16, :].astype(F32)[:, 0:8]
-        high = coarse_ref[part, width - 16 : width, :].astype(F32)[:, 8:16]
-        packed = pack_edges(low, high)
-        for k in range(2):
-            edge_out[0, k, pl.ds(pl.multiple_of(i * 32, 32), 32)] = packed[k]
+        pack_edges(coarse_ref, 0, i)
 
     row_out[0, 0] = coarse_ref[0:3]
     row_out[0, 1] = coarse_ref[height - 3 : height]
@@ -132,7 +158,7 @@
         def _():
             for copy in row_copies(0, k):
                 copy.start()
-    for copy in edge_copies(0, 0, height):
+    for copy in edge_copies(0, 0, 4):
         copy.start()
 
     @pl.loop(0, height // 8)
@@ -182,67 +208,74 @@
                 def _():
                     chunk_copy(row, owned, lat, owner - 1, 1).start()
 
+    for load in loads[1:]:
+        load.wait()
+
     for l in range(2):
         x = x_ref.at[l]
+        rows = step_rows[l]
+        blocks = TS // rows
         one = slice(l, l + 1)
         for k in range(49):
             for g in range(groups):
                 wb_ref[k, g] = jnp.broadcast_to(dw_ref[k // 7, k % 7, l : l + 1, 128 * g : 128 * g + 128], (8, 128))
 
         def place_edges():
-            for copy in edge_copies(l, 0, height):
+            for copy in edge_copies(l, 0, 4):
                 copy.wait()
 
-            @pl.loop(0, height // 8)
+            @pl.loop(0, 4)
             def _(i):
-                part = pl.ds(pl.multiple_of(i * 32, 32), 32)
-                place = pl.ds(3 + i * 8, 8)
-                after = edge_in[l, 0, part].astype(F32).reshape(4, 8, channels)
-                before = edge_in[l, 1, part].astype(F32).reshape(4, 8, channels)
-                after = jnp.stack([after, swap_halves(after)], 1).reshape(8, 8, channels)
-                before = jnp.stack([swap_halves(before), before], 1).reshape(8, 8, channels)
-                for g in range(groups):
-                    lanes = slice(128 * g, 128 * g + 128)
-                    x[g, place, COL0 + width : COL0 + width + 8, :] = after[:, :, lanes]
-                    x[g, place, 0:8, :] = before[:, :, lanes]
+                part = pl.ds(pl.multiple_of(i * CHUNK, CHUNK), CHUNK)
+                after = edge_in[l, 0, part].astype(F32)
+                before = edge_in[l, 1, part].astype(F32)
+                for t in range(3):
+                    after_blocks = [after[8 * n : 8 * n + 8] for n in range(3 * t, 3 * t + 3)]
+                    before_blocks = [before[8 * n : 8 * n + 8] for n in range(3 * t, 3 * t + 3)]
+                    for r in range(8):
+                        line = 3 + t * TS + i * 8 + r
+                        right_part = unpack_row(after_blocks, r, 0)
+                        left_part = unpack_row(before_blocks, r, 5)
+                        for g in range(groups):
+                            lanes = slice(128 * g, 128 * g + 128)
+                            x[g, line, COL0 + width : COL0 + width + 8, :] = right_part[:, lanes]
+                            x[g, line, 0:8, :] = left_part[:, lanes]
+
+        def place_rows():
+            for k, present in enumerate((has_up, has_down)):
+                receives = (has_down, has_up)[k]
+                place = height + 3 if k == 0 else 0
+
+                @pl.when(present)
+                def _():
+                    for copy in row_copies(l, k):
+                        copy.wait_send()
+
+                @pl.when(receives)
+                def _():
+                    for copy in row_copies(l, k):
+                        copy.wait_recv()
+                    middle = row_in[l, k].astype(F32)
+                    after = corner_in[l, k, 0].astype(F32)
+                    before = corner_in[l, k, 1].astype(F32)
+                    after = [after[8 * n : 8 * n + 8] for n in range(3)]
+                    before = [before[8 * n : 8 * n + 8] for n in range(3)]
+                    for g in range(groups):
+                        lanes = slice(128 * g, 128 * g + 128)
+                        x[g, place : place + 3, COL0 : COL0 + width, :] = middle[:, :, lanes]
+                        for r in range(3):
+                            n = r if k == 0 else r + 5
+                            x[g, place + r, COL0 + width : COL0 + width + 8, :] = unpack_row(after, n, 0)[:, lanes]
+                            x[g, place + r, 0:8, :] = unpack_row(before, n, 5)[:, lanes]
+
+                @pl.when(jnp.logical_not(receives))
+                def _():
+                    for g in range(groups):
+                        x[g, place : place + 3] = jnp.zeros((3, width + 16, 128), F32)
 
         if l == 1:
+            place_rows()
             place_edges()
-
-        for k, present in enumerate((has_up, has_down)):
-            receives = (has_down, has_up)[k]
-            place = height + 3 if k == 0 else 0
-
-            @pl.when(present)
-            def _():
-                for copy in row_copies(l, k):
-                    copy.wait_send()
-
-            @pl.when(receives)
-            def _():
-                for copy in row_copies(l, k):
-                    copy.wait_recv()
-                middle = row_in[l, k].astype(F32)
-                after = corner_in[l, k, 0].astype(F32).reshape(2, 8, channels)
-                before = corner_in[l, k, 1].astype(F32).reshape(2, 8, channels)
-                for g in range(groups):
-                    lanes = slice(128 * g, 128 * g + 128)
-                    x[g, place : place + 3, COL0 : COL0 + width, :] = middle[:, :, lanes]
-                    for r in range(3):
-                        n = r if k == 0 else r + 1
-                        right_part = after[n // 2, :, lanes]
-                        left_part = before[n // 2, :, lanes]
-                        if n % 2:
-                            right_part = swap_halves(right_part)
-                        else:
-                            left_part = swap_halves(left_part)
-                        x[g, place + r, COL0 + width : COL0 + width + 8, :] = right_part
-                        x[g, place + r, 0:8, :] = left_part
-
-            @pl.when(jnp.logical_not(receives))
-            def _():
-                for g in range(groups):
-                    x[g, place : place + 3] = jnp.zeros((3, width + 16, 128), F32)
 
         def depthwise(i, parts):
             @pl.loop(0, 2)
@@ -252,22 +285,31 @@
                                 tile * TS + i * rows, rows, groups, parts)
 
         if l == 0:
-            @pl.loop(0, blocks)
+            @pl.loop(1, blocks - 1)
             def _(i):
                 depthwise(i, (1, 2))
 
+            place_rows()
+
+            @pl.loop(0, 2)
+            def _(n):
+                depthwise(n * (blocks - 1), (1, 2))
+
             place_edges()
 
         @pl.loop(0, blocks)
         def _(step):
-            i = step if l == 0 else lax.rem(step + lon // 8, blocks)
+            if l == 0:
+                i = jnp.where(step < 2, step * (blocks - 1), step - 1)
+            else:
+                i = lax.rem(step + lon // 8 * 2 + 4 * lax.rem(lat, 2), blocks)
 
             depthwise(i, (0, 3) if l == 0 else (0, 1, 2, 3))
 
             @pl.loop(0, 2)
             def _(s):
                 depth = jnp.concatenate([d_ref[s, g, pl.ds(pl.multiple_of(i * rows, rows), rows)].reshape(rows * width, 128) for g in range(groups)], 1)
-                u_ref[s] = mix_block(depth, gain_ref[one], shift_ref[one], win_ref[l], bin_ref[one], wout_ref[l],
+                u_ref[s, 0:rows] = mix_block(depth, gain_ref[one], shift_ref[one], win_ref[l], bin_ref[one], wout_ref[l],
                                      bout_ref[one]).reshape(rows, width, channels)
 
             for t in range(3):
@@ -276,39 +318,34 @@
                 for g in range(groups):
                     lanes = slice(128 * g, 128 * g + 128)
                     if t == 1:
-                        update = jnp.where(m0 == 0, u_ref[0, :, :, lanes], u_ref[1, :, :, lanes])
+                        update = jnp.where(m0 == 0, u_ref[0, 0:rows, :, lanes], u_ref[1, 0:rows, :, lanes])
                     else:
-                        update = u_ref[t // 2, :, :, lanes]
+                        update = u_ref[t // 2, 0:rows, :, lanes]
                     field = x[g, place, COL0 : COL0 + width, :]
                     field = (field + (masks[t] * scale_ref[one, lanes]) * update).astype(BF16)
                     out_ref[pl.ds(row0, rows), :, lanes] = field
                     if l == 0:
                         x_ref[1, g, place, COL0 : COL0 + width, :] = field.astype(F32)
             if l == 0:
-                for t in range(3):
-                    row0 = pl.multiple_of(t * TS + i * rows, rows)
-                    low = out_ref[pl.ds(row0, rows), 0:16, :].astype(F32)[:, 0:8]
-                    high = out_ref[pl.ds(row0, rows), width - 16 : width, :].astype(F32)[:, 8:16]
-                    packed = pack_edges(low, high)
-                    for k in range(2):
-                        edge_out[1, k, pl.ds(pl.multiple_of(row0 * 4, 32), rows * 4)] = packed[k]
-                    for copy in edge_copies(1, row0, rows):
-                        copy.start()
+                pack_edges(out_ref, 1, i)
+                for copy in edge_copies(1, i, 1):
+                    copy.start()
+
+                @pl.when(step == 1)
+                def _():
+                    row_out[1, 0] = out_ref[0:3]
+                    row_out[1, 1] = out_ref[height - 3 : height]
+                    for k, present in enumerate((has_up, has_down)):
+                        @pl.when(present)
+                        def _():
+                            for copy in row_copies(1, k):
+                                copy.start()
             else:
                 @pl.loop(0, 3 * rows)
                 def _(n):
-                    t = lax.rem(n, 3)
-                    r = lax.rem(n // 3 * 5 + lon // 4, rows)
+                    t = lax.rem(n + lat, 3)
+                    r = lax.rem(n // 3 * 3 + lon // 2, rows)
                     send_row(t * TS + i * rows + r)
-
-        if l == 0:
-            row_out[1, 0] = out_ref[0:3]
-            row_out[1, 1] = out_ref[height - 3 : height]
-            for k, present in enumerate((has_up, has_down)):
-                @pl.when(present)
-                def _():
-                    for copy in row_copies(1, k):
-                        copy.start()
 
     far = (nlon - 1) * width
 
@@ -343,29 +380,36 @@
         own_copy(0, owned).wait()
 
 
-def section_call(tiles, coarse, dw, dwb, gain, shift, win, b_in, wout, bout, scale, rows=8):
+def section_call(tiles, coarse, dw, dwb, gain, shift, win, b_in, wout, bout, scale, step_rows=(8, 4)):
     height, width, channels = coarse.shape
     groups = channels // 128
     nlon = lax.axis_size("lon")
     owned = height // nlon
     vmem = pl.BlockSpec(memory_space=pltpu.VMEM)
+    hbm = pl.BlockSpec(memory_space=pl.ANY)
     dma = pltpu.SemaphoreType.DMA
+    rows = max(step_rows)
     return pl.pallas_call(
-        section_kernel,
+        functools.partial(section_kernel, step_rows),
         out_shape=jax.ShapeDtypeStruct((owned + 1, nlon * width, channels), BF16),
-        in_specs=[pl.BlockSpec(memory_space=pltpu.SMEM)] + [vmem] * 10,
+        in_specs=[pl.BlockSpec(memory_space=pltpu.SMEM), hbm, hbm, vmem, vmem, vmem, hbm, vmem, hbm, vmem, vmem],
         out_specs=pl.BlockSpec(memory_space=pl.ANY),
         scratch_shapes=[
+            pltpu.VMEM(coarse.shape, BF16),
+            pltpu.VMEM(dw.shape, F32),
+            pltpu.VMEM(win.shape, BF16),
+            pltpu.VMEM(wout.shape, BF16),
+            dma((4,)),
             pltpu.VMEM((2, groups, height + 6, width + 16, 128), F32),
             pltpu.VMEM((49, groups, 8, 128), F32),
             pltpu.VMEM((2, groups, TS, width, 128), F32),
             pltpu.VMEM((2, rows, width, channels), F32),
             pltpu.VMEM((height, width, channels), BF16),
-            pltpu.VMEM((2, 2, height * 4, channels), BF16),
-            pltpu.VMEM((2, 2, height * 4, channels), BF16),
+            pltpu.VMEM((2, 2, 4 * CHUNK, channels), BF16),
+            pltpu.VMEM((2, 2, 4 * CHUNK, channels), BF16),
             pltpu.VMEM((2, 2, 3, width, channels), BF16),
             pltpu.VMEM((2, 2, 3, width, channels), BF16),
-            pltpu.VMEM((2, 2, 2, 16, channels), BF16),
+            pltpu.VMEM((2, 2, 2, 32, channels), BF16),
             dma((2, 8)),
             dma((2, 8)),
             dma((owned + 1,)),

time: 104 us -> 95.6 us (0.919)
  the two profiles are of different devices: /device:TPU:31 before, /device:TPU:1 now
where the time goes in v4:
time: 95.6 us; the launch traced here: 95 us
  Pallas kernels  94.9 us (99%)
    pallas_call x1, Pallas kernels, section_call(): pl.pallas_call(functools.partial(section_kernel, step_rows), out_shape=ja...  84.5 us
    pallas_call x1, Pallas kernels, upsample_call(): pl.pallas_call(upsample_kernel, grid=(chunks,), out_shape=jax.ShapeDtypeS...  10.4 us

profile of v4, /device:TPU:1, one launch (start us, length us, event | category | flops | bytes accessed | tf_op | source)
XLA Modules:
  0.0 95.0 jit_solution(4599824353695716727)
XLA Ops:
  0.0 84.5 %shard_map.127.y_ref.next_ref = bf16[4,1024,384]{2,1,0:T(8,128)(2,1)} custom-call(s32[1,3]{1,0:T(1,128)} %bitcast.10, bf16[96,32,384]{2,1,0:T(8,128)(2,1)} %coarse_hbm.1, f32[7,7,2,384]{3,2,1,0:T(2,128)} %bitcast.9, f32[2,384]{1,0:T(2,128)} %dwb_ref.1, f32[2,384]{1,0:T(2,128)} %gain_ref.1, f32[2,384]{1,0:T(2,128)} %shift_ref.1, ...), custom_call_target="tpu_custom_call" | custom-call | flops 12000000000 | bytes 10000000 | tf_op jit(solution)/shard_map/pallas_call | solution.py:392
  84.5 10.4 %shard_map.128 = bf16[6,192,2048]{2,1,0:T(8,128)(2,1)} custom-call(bf16[4,1024,384]{2,1,0:T(8,128)(2,1)} %shard_map.127.y_ref.next_ref, bf16[4,1024,384]{2,1,0:T(8,128)(2,1)} %shard_map.127.y_ref.next_ref, bf16[9,192,384]{2,1,0:T(8,128)(2,1)} %bitcast.7, f32[1,192]{1,0:T(1,128)} %bitcast.8), custom_call_target="tpu_custom_call" | custom-call | tf_op jit(solution)/shard_map/pallas_call | solution.py:484

commit v5 on v4

--- a/solution.py
+++ b/solution.py
@@ -273,10 +273,6 @@
                     for g in range(groups):
                         x[g, place : place + 3] = jnp.zeros((3, width + 16, 128), F32)
 
-        if l == 1:
-            place_rows()
-            place_edges()
-
         def depthwise(i, parts):
             @pl.loop(0, 2)
             def _(s):
@@ -284,6 +280,22 @@
                 depthwise_block(x, wb_ref, dwb_ref, l, d_ref.at[s, :, pl.ds(pl.multiple_of(i * rows, rows), rows)],
                                 tile * TS + i * rows, rows, groups, parts)
 
+        early = 3
+
+        def block_of(step):
+            if l == 0:
+                return jnp.where(step < 2, step * (blocks - 1), step - 1)
+            return lax.rem(step + lon // 8 * 2 + 4 * lax.rem(lat, 2), blocks)
+
+        if l == 1:
+            place_rows()
+
+            @pl.loop(0, early)
+            def _(step):
+                depthwise(block_of(step), (1, 2))
+
+            place_edges()
+
         if l == 0:
             @pl.loop(1, blocks - 1)
             def _(i):
@@ -299,12 +311,17 @@
 
         @pl.loop(0, blocks)
         def _(step):
+            i = block_of(step)
             if l == 0:
-                i = jnp.where(step < 2, step * (blocks - 1), step - 1)
+                depthwise(i, (0, 3))
             else:
-                i = lax.rem(step + lon // 8 * 2 + 4 * lax.rem(lat, 2), blocks)
-
-            depthwise(i, (0, 3) if l == 0 else (0, 1, 2, 3))
+                @pl.when(step < early)
+                def _():
+                    depthwise(i, (0, 3))
+
+                @pl.when(step >= early)
+                def _():
+                    depthwise(i, (0, 1, 2, 3))
 
             @pl.loop(0, 2)
             def _(s):

time: 95.6 us -> 95.1 us (level)
  Pallas kernels: 94.9 us -> 93.7 us
    pallas_call x1, Pallas kernels: 84.5 us -> 83.3 us  [section_call(): pl.pallas_call(functools.partial(section_kernel, step_rows), out_shape=ja...]
where the time goes in v5:
time: 95.1 us; the launch traced here: 93.7 us
  Pallas kernels  93.7 us (99%)
    pallas_call x1, Pallas kernels, section_call(): pl.pallas_call(functools.partial(section_kernel, step_rows), out_shape=ja...  83.3 us
    pallas_call x1, Pallas kernels, upsample_call(): pl.pallas_call(upsample_kernel, grid=(chunks,), out_shape=jax.ShapeDtypeS...  10.4 us

profile of v5, /device:TPU:1, one launch (start us, length us, event | category | flops | bytes accessed | tf_op | source)
XLA Modules:
  0.0 93.7 jit_solution(12754859228217078725)
XLA Ops:
  0.0 83.3 %shard_map.127.y_ref.next_ref = bf16[4,1024,384]{2,1,0:T(8,128)(2,1)} custom-call(s32[1,3]{1,0:T(1,128)} %bitcast.10, bf16[96,32,384]{2,1,0:T(8,128)(2,1)} %coarse_hbm.1, f32[7,7,2,384]{3,2,1,0:T(2,128)} %bitcast.9, f32[2,384]{1,0:T(2,128)} %dwb_ref.1, f32[2,384]{1,0:T(2,128)} %gain_ref.1, f32[2,384]{1,0:T(2,128)} %shift_ref.1, ...), custom_call_target="tpu_custom_call" | custom-call | flops 12000000000 | bytes 10000000 | tf_op jit(solution)/shard_map/pallas_call | solution.py:409
  83.3 10.4 %shard_map.128 = bf16[6,192,2048]{2,1,0:T(8,128)(2,1)} custom-call(bf16[4,1024,384]{2,1,0:T(8,128)(2,1)} %shard_map.127.y_ref.next_ref, bf16[4,1024,384]{2,1,0:T(8,128)(2,1)} %shard_map.127.y_ref.next_ref, bf16[9,192,384]{2,1,0:T(8,128)(2,1)} %bitcast.7, f32[1,192]{1,0:T(1,128)} %bitcast.8), custom_call_target="tpu_custom_call" | custom-call | tf_op jit(solution)/shard_map/pallas_call | solution.py:501

commit v6 on v5

--- a/solution.py
+++ b/solution.py
@@ -280,7 +280,7 @@
                 depthwise_block(x, wb_ref, dwb_ref, l, d_ref.at[s, :, pl.ds(pl.multiple_of(i * rows, rows), rows)],
                                 tile * TS + i * rows, rows, groups, parts)
 
-        early = 3
+        early = 5
 
         def block_of(step):
             if l == 0:

time: 95.1 us -> 96 us (level)
  the two profiles are of different devices: /device:TPU:1 before, /device:TPU:17 now
where the time goes in v6:
time: 96 us; the launch traced here: 95.9 us
  Pallas kernels  95.9 us (100%)
    pallas_call x1, Pallas kernels, section_call(): pl.pallas_call(functools.partial(section_kernel, step_rows), out_shape=ja...  85.4 us
    pallas_call x1, Pallas kernels, upsample_call(): pl.pallas_call(upsample_kernel, grid=(chunks,), out_shape=jax.ShapeDtypeS...  10.4 us

profile of v6, /device:TPU:17, one launch (start us, length us, event | category | flops | bytes accessed | tf_op | source)
XLA Modules:
  0.0 95.9 jit_solution(10679372993615715356)
XLA Ops:
  0.0 85.4 %shard_map.127.y_ref.next_ref = bf16[4,1024,384]{2,1,0:T(8,128)(2,1)} custom-call(s32[1,3]{1,0:T(1,128)} %bitcast.10, bf16[96,32,384]{2,1,0:T(8,128)(2,1)} %coarse_hbm.1, f32[7,7,2,384]{3,2,1,0:T(2,128)} %bitcast.9, f32[2,384]{1,0:T(2,128)} %dwb_ref.1, f32[2,384]{1,0:T(2,128)} %gain_ref.1, f32[2,384]{1,0:T(2,128)} %shift_ref.1, ...), custom_call_target="tpu_custom_call" | custom-call | flops 12000000000 | bytes 10000000 | tf_op jit(solution)/shard_map/pallas_call | solution.py:409
  85.4 10.4 %shard_map.128 = bf16[6,192,2048]{2,1,0:T(8,128)(2,1)} custom-call(bf16[4,1024,384]{2,1,0:T(8,128)(2,1)} %shard_map.127.y_ref.next_ref, bf16[4,1024,384]{2,1,0:T(8,128)(2,1)} %shard_map.127.y_ref.next_ref, bf16[9,192,384]{2,1,0:T(8,128)(2,1)} %bitcast.7, f32[1,192]{1,0:T(1,128)} %bitcast.8), custom_call_target="tpu_custom_call" | custom-call | tf_op jit(solution)/shard_map/pallas_call | solution.py:501
